TPU v7x, 32 devices: a whole 2x2x4 slice. The times are simulated.
32 devices in a mesh: grp: 2 (over y), src: 4 (over z), rcv: 2 (over x), tim: 2 (over core).
Axes of the slice: x: 2, y: 2, z: 4, core: 2. Of those that a mesh axis runs over, the one named last changes fastest.
Arguments:
- response: bfloat16 [2048, 128, 2048], P('src', 'tim', 'rcv'), may hold values from -80 to 80, as said below
- onset: int32 [2048, 2048], P('src', 'rcv'), may hold values from 0 to 127
- direct_wave: bfloat16 [4096, 256], P(('grp', 'rcv'), 'src'), parts along dimension 0, may hold values from -6 to 6
- arrival: int32 [4096], P('grp'), parts along dimension 0, may hold values from 64 to 255
Outputs:
- focus_down: bfloat16 [4096, 256], P(('grp', 'rcv'), 'src'), parts along dimension 0
- focus_up: bfloat16 [4096, 256], P(('grp', 'src')), parts along dimension 0
There are 2 independent parts, one for each index of `grp`. A program takes and returns all parts, laid end to end along the dimension named above; an argument that names none is the same for every part. Nothing has to cross between parts.
Inputs may be any that keep to these rules, and one draw needn't show every extreme that they name: response is a reflection response in the printed table's range.
All inputs are finite; a program needn't handle non-finite values.
Results may differ from a plain program's by a relative error of at most 0.015.
Values may be sent and summed in bfloat16 or wider, within the bound.
No kernel may reach another device: no remote copies, remote signals or barrier semaphores. Data moves between devices by JAX's collectives and lax.ppermute only.
A program may use at most 320 MiB of HBM per device.

v0:
```python
import jax
import jax.numpy as jnp
from jax import lax
from jax.sharding import PartitionSpec as P

STATIONS = 2048
ITERS = 2


def delay_sum(product, offset):
    row_count, taps_here, time_span = product.shape
    row_width = time_span + taps_here
    padded = jnp.pad(product, ((0, 0), (0, 0), (0, taps_here)))
    flattened = padded.reshape(row_count, taps_here * row_width)[:, : taps_here * (row_width - 1)]
    sheared = flattened.reshape(row_count, taps_here, row_width - 1)
    summed = jnp.sum(sheared, axis=1)[:, :time_span]
    framed = jnp.concatenate([jnp.zeros((row_count, time_span), jnp.float32), summed], axis=1)
    return lax.dynamic_slice_in_dim(framed, time_span - offset, time_span, 1)


def advance_stack(series, taps_here, offset):
    row_count, time_span = series.shape
    framed = jnp.concatenate([series, jnp.zeros((row_count, time_span), series.dtype)], axis=1)
    row_width = time_span + taps_here
    advanced = lax.dynamic_slice_in_dim(framed, offset, row_width, 1)
    repeated = jnp.broadcast_to(advanced[:, None, :], (row_count, taps_here, row_width))
    repeated = repeated.reshape(row_count, taps_here * row_width)
    repeated = jnp.pad(repeated, ((0, 0), (0, taps_here)))
    return repeated.reshape(row_count, taps_here, row_width + 1)[:, :, :time_span]


def on_device(response, onset, direct_wave, arrival):
    src_rows, tap_rows, rcv_rows = response.shape
    tile_time = direct_wave.shape[1]
    tap_start = lax.axis_index("tim") * tap_rows
    tap_index = tap_start + lax.broadcasted_iota(jnp.int32, (1, tap_rows, 1), 1)
    kept_resp = jnp.where(tap_index >= onset[:, None, :], response, jnp.zeros((), response.dtype))
    energy = lax.psum(jnp.sum(jnp.square(response.astype(jnp.float32))), ("src", "rcv", "tim"))
    unit_gain = lax.rsqrt(energy / STATIONS + 1e-06)
    src_arrival = lax.dynamic_slice_in_dim(arrival, lax.axis_index("src") * src_rows, src_rows)
    rcv_arrival = lax.dynamic_slice_in_dim(arrival, lax.axis_index("rcv") * rcv_rows, rcv_rows)
    whole_field = lax.all_gather(direct_wave, "src", axis=1, tiled=True)
    current = whole_field
    focus_down = direct_wave
    focus_up = None
    for iteration in range(ITERS):
        final_pass = iteration + 1 == ITERS
        product = lax.dot_general(
            kept_resp, current, (((2,), (0,)), ((), ())), preferred_element_type=jnp.float32
        )
        partial_value = delay_sum(product, tap_start)
        up_share = lax.psum_scatter(
            partial_value.astype(jnp.bfloat16), ("rcv", "tim"), scatter_dimension=1, tiled=True
        ).astype(jnp.float32)
        share_width = up_share.shape[1]
        share_start = (
            lax.axis_index("rcv") * lax.axis_size("tim") + lax.axis_index("tim")
        ) * share_width
        share_index = share_start + lax.broadcasted_iota(jnp.int32, (1, share_width), 1)
        up_piece = jnp.where(share_index < src_arrival[:, None], unit_gain * up_share, 0.0).astype(
            jnp.bfloat16
        )
        focus_up = lax.all_gather(up_piece, ("rcv", "tim"), axis=1, tiled=True)
        stacked = advance_stack(focus_up, tap_rows, tap_start)
        backward_sum = lax.dot_general(
            kept_resp, stacked, (((0, 1), (0, 1)), ((), ())), preferred_element_type=jnp.float32
        )
        field_share = lax.psum_scatter(
            backward_sum, ("src", "tim"), scatter_dimension=1, tiled=True
        )
        share_width = field_share.shape[1]
        local_start = lax.axis_index("tim") * share_width
        share_index = (
            lax.axis_index("src") * tile_time
            + local_start
            + lax.broadcasted_iota(jnp.int32, (1, share_width), 1)
        )
        direct_part = lax.dynamic_slice_in_dim(direct_wave, local_start, share_width, 1)
        field_piece = (
            direct_part.astype(jnp.float32)
            + jnp.where(share_index < rcv_arrival[:, None], unit_gain * field_share, 0.0)
        ).astype(jnp.bfloat16)
        if final_pass:
            focus_down = lax.all_gather(field_piece, "tim", axis=1, tiled=True)
        else:
            current = lax.all_gather(field_piece, ("src", "tim"), axis=1, tiled=True)
    return (focus_down, focus_up)


def solution(mesh):
    in_specs = (P("src", "tim", "rcv"), P("src", "rcv"), P(("grp", "rcv"), "src"), P("grp"))
    out_specs = (P(("grp", "rcv"), "src"), P(("grp", "src"), None))
    return jax.shard_map(
        on_device, mesh=mesh, in_specs=in_specs, out_specs=out_specs, check_vma=False
    )
```

profile of v0, /device:TPU:0, one launch (start us, length us, event | category | flops | bytes accessed | tf_op | source)
XLA Modules:
  0.0 828.2 jit_solution(13086828196339413014)
XLA Ops:
  7.2 17.6 %all_gather.15 = bf16[1024,256]{0,1:T(8,128)(2,1)S(1)} all-gather(bf16[1024,64]{0,1:T(8,128)(2,1)} %param.6), channel_id=1, replica_groups=mesh['grp'=2,'src'=4,'rcv'=2,'tim'=2] {'src'}, dimensions={1}, use_global_device_ids=true | all-gather | bytes 655360 | tf_op jit(solution)/shard_map/all_gather | solution.py:42
  24.8 45.3 %compare_select_fusion = bf16[512,64,1024]{2,1,0:T(8,128)(2,1)} fusion(bf16[512,64,1024]{2,1,0:T(8,128)(2,1)} %param.4, s32[512,1024]{1,0:T(8,128)} %param.5, s32[64]{0:T(128)S(1)} %iota_add_fusion.1), kind=kLoop, calls=%fused_computation.1 | loop fusion | flops 67108864 | bytes 136315136 | tf_op jit(solution)/shard_map/jit(_where)/select_n | solution.py:37
  70.1 73.0 %fusion = f32[512,64,256]{0,2,1:T(8,128)} fusion(bf16[512,64,1024]{2,1,0:T(8,128)(2,1)} %compare_select_fusion, bf16[1024,256]{0,1:T(8,128)(2,1)S(1)} %all_gather.15), kind=kOutput, calls=%fused_computation.2 | convolution fusion | flops 17179869184 | bytes 101187584 | tf_op jit(solution)/shard_map/dot_general | solution.py:48
  143.1 26.1 %pad.18 = f32[512,64,320]{0,2,1:T(8,128)} pad(f32[512,64,256]{0,2,1:T(8,128)} %fusion, f32[]{:T(128)} %constant.34.clone.1), padding=0_0x0_0x0_64 | pad | bytes 75497472 | tf_op jit(solution)/shard_map/jit(_pad)/pad | solution.py:13
  169.2 28.4 %slice.24 = f32[512,20416]{0,1:T(8,128)} slice(f32[512,20480]{0,1:T(8,128)} %bitcast.34), slice={[0:512], [0:20416]} | slice | bytes 83623936 | tf_op jit(solution)/shard_map/slice | solution.py:14
  197.6 43.7 %reshape.49 = f32[512,64,319]{0,2,1:T(8,128)} reshape(f32[512,20416]{0,1:T(8,128)} %slice.24) | data formatting | bytes 83623936 | tf_op jit(solution)/shard_map/reshape | solution.py:15
  241.3 15.1 %reduce_sum.28 = bf16[512,319]{0,1:T(8,128)(2,1)S(1)} reduce(f32[512,64,319]{0,2,1:T(8,128)} %reshape.49, f32[]{:T(128)} %constant.34.clone.1), dimensions={1}, to_apply=%region_2.3 | reduce | flops 10289664 | bytes 42138628 | tf_op jit(solution)/shard_map/reduce_sum | solution.py:16
  257.4 37.0 %multiply_reduce_fusion = f32[]{:T(128)} fusion(bf16[512,64,1024]{2,1,0:T(8,128)(2,1)} %param.4), kind=kLoop, calls=%fused_computation | loop fusion | flops 100663296 | bytes 67108864 | tf_op jit(solution)/shard_map/reduce_sum | solution.py:38
  294.4 30.9 %psum.7 = f32[]{:T(128)} all-reduce(f32[]{:T(128)} %multiply_reduce_fusion), channel_id=1, replica_groups=mesh['grp'=2,'src'=4,'rcv'=2,'tim'=2] {'src','rcv','tim'}, use_global_device_ids=true, to_apply=%region_1.2 | all-reduce | flops 1 | bytes 8 | tf_op jit(solution)/shard_map/psum | solution.py:38
  343.9 18.2 %reshape.51 = bf16[512,64,321]{0,2,1:T(8,128)(2,1)} reshape(bf16[512,20544]{0,1:T(8,128)(2,1)} %pad.19) | data formatting | bytes 42074112 | tf_op jit(solution)/shard_map/reshape | solution.py:29
  375.9 23.4 %copy.37 = bf16[512,64,256]{2,1,0:T(8,128)(2,1)} copy(bf16[512,64,256]{0,2,1:T(8,128)(2,1)} %slice.26) | data formatting | bytes 33554432
  399.3 30.9 %convolution_bitcast_fusion.1 = f32[1024,256]{0,1:T(8,128)} fusion(bf16[512,64,1024]{2,1,0:T(8,128)(2,1)} %compare_select_fusion, bf16[512,64,256]{2,1,0:T(8,128)(2,1)} %copy.37), kind=kOutput, calls=%fused_computation.7 | convolution fusion | flops 17179869184 | bytes 84934656 | tf_op jit(solution)/shard_map/dot_general | solution.py:65
  430.3 29.7 %reduce-scatter.9.cloned.1.call-done = f32[1024,32]{0,1:T(8,128)} async-done(((f32[1024,256]{0,1:T(8,128)}), f32[1024,32]{0,1:T(8,128)}) %reduce-scatter.9.cloned.1.call-update) | async-done | bytes 131088 | tf_op jit(solution)/shard_map/reduce_scatter | solution.py:68
  461.0 15.2 %all_gather.17 = bf16[1024,256]{0,1:T(8,128)(2,1)S(1)} all-gather(bf16[1024,32]{0,1:T(8,128)(2,1)S(1)} %fusion.10), channel_id=1, replica_groups=mesh['grp'=2,'src'=4,'rcv'=2,'tim'=2] {'src','tim'}, dimensions={1}, use_global_device_ids=true | all-gather | bytes 589824 | tf_op jit(solution)/shard_map/all_gather | solution.py:86
  476.2 73.0 %fusion.2 = f32[512,64,256]{0,2,1:T(8,128)} fusion(bf16[512,64,1024]{2,1,0:T(8,128)(2,1)} %compare_select_fusion, bf16[1024,256]{0,1:T(8,128)(2,1)S(1)} %all_gather.17), kind=kOutput, calls=%fused_computation.4 | convolution fusion | flops 17179869184 | bytes 101187584 | tf_op jit(solution)/shard_map/dot_general | solution.py:48
  549.2 26.1 %pad.20 = f32[512,64,320]{0,2,1:T(8,128)} pad(f32[512,64,256]{0,2,1:T(8,128)} %fusion.2, f32[]{:T(128)} %constant.34.clone.1), padding=0_0x0_0x0_64 | pad | bytes 75497472 | tf_op jit(solution)/shard_map/jit(_pad)/pad | solution.py:13
  575.4 28.4 %slice.27 = f32[512,20416]{0,1:T(8,128)} slice(f32[512,20480]{0,1:T(8,128)} %bitcast.35), slice={[0:512], [0:20416]} | slice | bytes 83623936 | tf_op jit(solution)/shard_map/slice | solution.py:14
  603.7 43.7 %reshape.53 = f32[512,64,319]{0,2,1:T(8,128)} reshape(f32[512,20416]{0,1:T(8,128)} %slice.27) | data formatting | bytes 83623936 | tf_op jit(solution)/shard_map/reshape | solution.py:15
  647.4 15.1 %reduce_sum.29 = bf16[512,319]{0,1:T(8,128)(2,1)S(1)} reduce(f32[512,64,319]{0,2,1:T(8,128)} %reshape.53, f32[]{:T(128)} %constant.34.clone.1), dimensions={1}, to_apply=%region_5.6 | reduce | flops 10289664 | bytes 42138628 | tf_op jit(solution)/shard_map/reduce_sum | solution.py:16
  663.5 17.9 %reduce-scatter.15.cloned.1.call-done = bf16[64,512]{1,0:T(8,128)(2,1)} async-done(((bf16[256,512]{1,0:T(8,128)(2,1)}), bf16[64,512]{1,0:T(8,128)(2,1)}) %reduce-scatter.15.cloned.1.call-update) | async-done | bytes 65552
  699.3 18.2 %reshape.55 = bf16[512,64,321]{0,2,1:T(8,128)(2,1)} reshape(bf16[512,20544]{0,1:T(8,128)(2,1)} %pad.21) | data formatting | bytes 42074112 | tf_op jit(solution)/shard_map/reshape | solution.py:29
  731.2 23.4 %copy.38 = bf16[512,64,256]{2,1,0:T(8,128)(2,1)} copy(bf16[512,64,256]{0,2,1:T(8,128)(2,1)} %slice.29) | data formatting | bytes 33554432
  754.6 30.9 %convolution_bitcast_fusion = f32[1024,256]{0,1:T(8,128)} fusion(bf16[512,64,1024]{2,1,0:T(8,128)(2,1)} %compare_select_fusion, bf16[512,64,256]{2,1,0:T(8,128)(2,1)} %copy.38), kind=kOutput, calls=%fused_computation.6 | convolution fusion | flops 17179869184 | bytes 84934656 | tf_op jit(solution)/shard_map/dot_general | solution.py:65
  786.4 31.7 %reduce-scatter.11.cloned.1.call-done = f32[1024,32]{0,1:T(8,128)} async-done(((f32[1024,256]{0,1:T(8,128)}), f32[1024,32]{0,1:T(8,128)}) %reduce-scatter.11.cloned.1.call-update) | async-done | bytes 131088 | tf_op jit(solution)/shard_map/reduce_scatter | solution.py:68
  (57 shorter events, 70.6 us)
Async XLA Ops:
  7.2 319.0 %reduce-scatter.13.cloned.1.call-start = ((), (), s32[]{:S(2)}) async-start(), calls=%async_computation.6 | async-start | bytes 327680
  256.4 69.6 %copy-start.6 = (s32[2048]{0:T(1024)S(1)}, s32[2048]{0:T(1024)}, u32[]{:S(2)}) copy-start(s32[2048]{0:T(1024)} %param.7) | copy-start | bytes 24580
  257.3 202.7 %reduce-scatter.9.cloned.1.call-start = ((), (), s32[]{:S(2)}) async-start(), calls=%async_computation.4 | async-start | bytes 1179648 | tf_op jit(solution)/shard_map/reduce_scatter | solution.py:68
  326.1 36.0 %copy-start.4 = (s32[512]{0:T(512)}, s32[512]{0:T(512)S(1)}, u32[]{:S(2)}) copy-start(s32[512]{0:T(512)S(1)} %dynamic_slice.24) | copy-start | bytes 6148
  326.1 36.0 %copy-start.7 = (s32[64]{0:T(128)}, s32[64]{0:T(128)S(1)}, u32[]{:S(2)}) copy-start(s32[64]{0:T(128)S(1)} %iota_add_fusion) | copy-start | bytes 772
  399.3 60.7 %copy-start = (bf16[1024,64]{0,1:T(8,128)(2,1)S(1)}, bf16[1024,64]{0,1:T(8,128)(2,1)}, u32[]{:S(2)}) copy-start(bf16[1024,64]{0,1:T(8,128)(2,1)} %param.6) | copy-start | bytes 393220
  430.2 251.2 %reduce-scatter.15.cloned.1.call-start = ((), (), s32[]{:S(2)}) async-start(), calls=%async_computation.7 | async-start | bytes 327680
  430.3 119.0 %copy-start.2 = (s32[1024]{0:T(1024)}, s32[1024]{0:T(1024)S(1)}, u32[]{:S(2)}) copy-start(s32[1024]{0:T(1024)S(1)} %dynamic_slice.23) | copy-start | bytes 12292
  430.3 119.0 %copy-start.9 = (s32[32]{0:T(128)}, s32[32]{0:T(128)S(1)}, u32[]{:S(2)}) copy-start(s32[32]{0:T(128)S(1)} %iota_add_fusion.2) | copy-start | bytes 388
  647.4 34.0 %copy-start.5 = (s32[512]{0:T(512)S(1)}, s32[512]{0:T(512)}, u32[]{:S(2)}) copy-start(s32[512]{0:T(512)} %copy-done.4) | copy-start | bytes 6148
  647.4 34.0 %copy-start.8 = (s32[64]{0:T(128)S(1)}, s32[64]{0:T(128)}, u32[]{:S(2)}) copy-start(s32[64]{0:T(128)} %copy-done.7) | copy-start | bytes 772
  663.5 154.6 %reduce-scatter.11.cloned.1.call-start = ((), (), s32[]{:S(2)}) async-start(), calls=%async_computation.5 | async-start | bytes 1179648 | tf_op jit(solution)/shard_map/reduce_scatter | solution.py:68
  754.6 63.5 %copy-start.1 = (bf16[1024,64]{0,1:T(8,128)(2,1)S(1)}, bf16[1024,64]{0,1:T(8,128)(2,1)}, u32[]{:S(2)}) copy-start(bf16[1024,64]{0,1:T(8,128)(2,1)} %param.6) | copy-start | bytes 393220
  754.6 63.5 %copy-start.3 = (s32[1024]{0:T(1024)S(1)}, s32[1024]{0:T(1024)}, u32[]{:S(2)}) copy-start(s32[1024]{0:T(1024)} %copy-done.2) | copy-start | bytes 12292
  754.6 63.5 %copy-start.10 = (s32[32]{0:T(128)S(1)}, s32[32]{0:T(128)}, u32[]{:S(2)}) copy-start(s32[32]{0:T(128)} %copy-done.9) | copy-start | bytes 388
Sparse Core Ops, SparseCore 0:
  257.4 21.7 reduce-scatter.12
  430.3 29.6 reduce-scatter.8
  663.6 17.7 reduce-scatter.14
  785.6 32.4 reduce-scatter.10
where the time goes:
time: 831 us; the launch traced here: 828 us
  local copies, waits for them, and re-layouts  332 us (40%)
  matrix products  208 us (25%)
  other arithmetic  116 us (14%)
  waiting for transfers between devices  79.4 us (10%)
  blocking collectives  77.6 us (9%)
  between operations  14.6 us (2%)
    dot_general x2, matrix products, on_device(): lax.dot_general(kept_resp, current, (((2,), (0,)), ((), ())), preferred_e...  146 us
    reshape x2, local copies, waits for them, and re-layouts, delay_sum(): sheared = flattened.reshape(row_count, taps_here, row_width - 1)  87.4 us
    dot_general x2, matrix products, on_device(): lax.dot_general(kept_resp, stacked, (((0, 1), (0, 1)), ((), ())), preferr...  61.7 us
    reduce_scatter x2, waiting for transfers between devices, on_device(): lax.psum_scatter(backward_sum, ('src', 'tim'), scatter_dimension=1, tiled...  61.5 us
    slice x2, local copies, waits for them, and re-layouts, delay_sum(): padded.reshape(row_count, taps_here * row_width)  56.7 us
    pad x2, local copies, waits for them, and re-layouts, delay_sum(): padded = jnp.pad(product, ((0, 0), (0, 0), (0, taps_here)))  52.2 us
    unnamed x28, local copies, waits for them, and re-layouts  50 us
    select_n x1, other arithmetic, on_device(): jnp.where(tap_index >= onset[:, None, :], response, jnp.zeros((), respons...  45.3 us
  transfers between devices with their start and end apart: 4, of which 3 were waited for; matrix products, arithmetic and copies ran while one was open for 5% of the time, Pallas kernels for 0%

commit v1 on v0

v1 whole, which is shorter than its diff:
```python
import functools

import jax
import jax.numpy as jnp
from jax import lax
from jax.experimental import pallas as pl
from jax.experimental.pallas import tpu as pltpu
from jax.sharding import PartitionSpec as P

STATIONS = 2048
ITERS = 2
MIB = 1 << 20
bf16 = jnp.bfloat16
f32 = jnp.float32
VM = pl.BlockSpec(memory_space=pltpu.VMEM)
SM = pl.BlockSpec(memory_space=pltpu.SMEM)
ANY = pl.BlockSpec(memory_space=pl.ANY)


def load_kernel(pos_ref, r_hbm, on_hbm, k_ref, e_out, on_ref, e_ref, sem, *, chunks, sub):
    rows, taps, cols = k_ref.shape
    size = rows // chunks
    start = pl.multiple_of(pos_ref[0], 8)
    tap_start = pos_ref[1]

    def part(c):
        return pltpu.make_async_copy(
            r_hbm.at[pl.ds(start + c * size, size)], k_ref.at[pl.ds(c * size, size)], sem.at[c]
        )

    onset_copy = pltpu.make_async_copy(on_hbm.at[pl.ds(start, rows)], on_ref, sem.at[chunks])
    onset_copy.start()
    for c in range(chunks):
        part(c).start()
    e_ref[...] = jnp.zeros_like(e_ref)
    tap = lax.broadcasted_iota(jnp.int32, (1, taps, 1), 1).astype(f32).astype(bf16)
    onset_copy.wait()
    for c in range(chunks):
        part(c).wait()

        def body(b, carry):
            at = pl.multiple_of(c * size + b * sub, sub)
            r = k_ref[pl.ds(at, sub)]
            x = r.astype(f32)
            e_ref[...] += jnp.sum((x * x).reshape(sub * taps // 8, 8, cols), axis=0)
            on = (on_ref[pl.ds(at, sub)] - tap_start).astype(f32).astype(bf16)
            keep = jnp.broadcast_to(tap, r.shape) >= on[:, None, :]
            k_ref[pl.ds(at, sub)] = jnp.where(keep, r, jnp.zeros((), bf16))
            return carry

        lax.fori_loop(0, size // sub, body, 0)
    e_out[0] = jnp.sum(e_ref[...])


def load_kept(pos, response, onset, rows):
    _, taps, cols = response.shape
    sub = 8
    chunks = max(1, min(16, rows // sub))
    return pl.pallas_call(
        functools.partial(load_kernel, chunks=chunks, sub=sub),
        in_specs=[SM, ANY, ANY],
        out_specs=[VM, SM],
        out_shape=[pltpu.VMEM((rows, taps, cols), bf16), jax.ShapeDtypeStruct((1,), f32)],
        scratch_shapes=[
            pltpu.VMEM((rows, cols), jnp.int32),
            pltpu.VMEM((8, cols), f32),
            pltpu.SemaphoreType.DMA((chunks + 1,)),
        ],
        compiler_params=pltpu.CompilerParams(vmem_limit_bytes=14 * MIB),
        cost_estimate=pl.CostEstimate(
            flops=0, bytes_accessed=rows * taps * cols * 2, transcendentals=0
        ),
        name="load_kept",
    )(pos, response, onset)


def steps_of(rows):
    sub = min(16, rows)
    unroll = 2 if rows % (2 * sub) == 0 else 1
    return sub, unroll


def forward_kernel(pos_ref, k_ref, f_ref, o_ref, *, first, groups):
    taps, cols = k_ref.shape[1:]
    rows = o_ref.shape[0]
    time = f_ref.shape[0] // groups
    sub, unroll = steps_of(rows)
    tap_start = pos_ref[1]
    sample = lax.broadcasted_iota(jnp.int32, (8, time), 0) + lax.broadcasted_iota(
        jnp.int32, (8, time), 1
    )

    def body(step, carry):
        for u in range(unroll):
            at = pl.multiple_of((step * unroll + u) * sub, sub)
            k = k_ref[pl.ds(first + at, sub)].reshape(sub * taps, cols)
            p = lax.dot_general(
                k, f_ref[...], (((1,), (1,)), ((), ())), preferred_element_type=f32
            )
            p = p.reshape(sub, taps // 8, 8, groups * time)
            for g in range(groups):
                total = None
                for j in range(taps // 8 - 1, -1, -1):
                    inside = (sample < time - tap_start - 8 * j)[None]
                    term = jnp.where(inside, p[:, j, :, g * time : (g + 1) * time], 0.0)
                    total = term if total is None else pltpu.roll(total, 8, 2) + term
                total = pltpu.roll(total, 0, 2, stride=1, stride_axis=1)
                o_ref[pl.ds(at, sub), g * time : (g + 1) * time] = pltpu.roll(
                    jnp.sum(total, axis=1), tap_start, 1
                )
        return carry

    lax.fori_loop(0, rows // (sub * unroll), body, 0)


def forward(pos, kept, field, first, rows, groups):
    _, taps, cols = kept.shape
    width = field.shape[0]
    return pl.pallas_call(
        functools.partial(forward_kernel, first=first, groups=groups),
        in_specs=[SM, VM, VM],
        out_specs=VM,
        out_shape=jax.ShapeDtypeStruct((rows, width), f32),
        compiler_params=pltpu.CompilerParams(vmem_limit_bytes=24 * MIB),
        cost_estimate=pl.CostEstimate(
            flops=2 * rows * taps * cols * width, bytes_accessed=width * cols * 2, transcendentals=0
        ),
        name="forward",
    )(pos, pltpu.with_memory_space_constraint(kept, pltpu.VMEM), field)


def backward_kernel(pos_ref, k_ref, u_ref, *refs, first, groups):
    before_ref, (o_ref, acc_ref) = (refs[0] if len(refs) == 3 else None), refs[-2:]
    taps, cols = k_ref.shape[1:]
    rows = u_ref.shape[0]
    time = u_ref.shape[1] // groups
    sub, unroll = steps_of(rows)
    tap_start = pos_ref[1]
    sample = lax.broadcasted_iota(jnp.int32, (8, time), 0) + lax.broadcasted_iota(
        jnp.int32, (8, time), 1
    )
    acc_ref[...] = jnp.zeros_like(acc_ref) if before_ref is None else before_ref[...]

    def body(step, carry):
        for n in range(unroll):
            at = pl.multiple_of((step * unroll + n) * sub, sub)
            k = k_ref[pl.ds(first + at, sub)].reshape(sub * taps, cols)
            stacks = []
            for g in range(groups):
                u = u_ref[pl.ds(at, sub), g * time : (g + 1) * time].astype(f32)
                u = pltpu.roll(u, time - tap_start, 1)
                base = jnp.stack([pltpu.roll(u, time - i, 1) if i else u for i in range(8)], axis=1)
                terms = []
                for j in range(taps // 8):
                    moved = pltpu.roll(base, time - 8 * j, 2) if j else base
                    inside = (sample < time - tap_start - 8 * j)[None]
                    terms.append(jnp.where(inside, moved, 0.0))
                stacks.append(jnp.stack(terms, 1).astype(bf16).reshape(sub * taps, time))
            stacked = jnp.concatenate(stacks, axis=1)
            acc_ref[...] += lax.dot_general(
                stacked, k, (((0,), (0,)), ((), ())), preferred_element_type=f32
            )
        return carry

    lax.fori_loop(0, rows // (sub * unroll), body, 0)
    o_ref[...] = acc_ref[...].astype(o_ref.dtype)


def backward(pos, kept, up, before, first, groups, kind):
    _, taps, cols = kept.shape
    rows, width = up.shape
    more = [] if before is None else [before]
    return pl.pallas_call(
        functools.partial(backward_kernel, first=first, groups=groups),
        in_specs=[SM, VM, VM] + [VM] * len(more),
        out_specs=VM,
        out_shape=jax.ShapeDtypeStruct((width, cols), kind),
        scratch_shapes=[pltpu.VMEM((width, cols), f32)],
        compiler_params=pltpu.CompilerParams(vmem_limit_bytes=24 * MIB),
        cost_estimate=pl.CostEstimate(
            flops=2 * rows * taps * cols * width, bytes_accessed=width * cols * 4, transcendentals=0
        ),
        name="backward",
    )(pos, pltpu.with_memory_space_constraint(kept, pltpu.VMEM), up, *more)


def shifted(x, axis, shift):
    n = lax.axis_size(axis)
    return lax.ppermute(x, axis, [(i, (i + shift) % n) for i in range(n)])


def gather(x, axis):
    n = lax.axis_size(axis)
    if n == 1:
        return x[None]
    if n > 8:
        return lax.all_gather(x, axis)
    got = [x] + [shifted(x, axis, -k) for k in range(1, n)]
    ring = jnp.stack(got + got[:-1])
    return lax.dynamic_slice_in_dim(ring, (n - lax.axis_index(axis)) % n, n, 0)


def scatter_parts(x, axis):
    n = lax.axis_size(axis)
    me = lax.axis_index(axis)
    if n == 1:
        return [x[0]]
    if n > 8:
        got = lax.all_to_all(x, axis, 0, 0, tiled=True)
        return [got[i] for i in range(n)]
    parts = [lax.dynamic_index_in_dim(x, me, 0, False)]
    for k in range(1, n):
        parts.append(shifted(lax.dynamic_index_in_dim(x, (me + k) % n, 0, False), axis, k))
    return parts


def total_of(parts):
    total = parts[0].astype(f32)
    for part in parts[1:]:
        total = total + part.astype(f32)
    return total


def on_device(response, onset, direct_wave, arrival):
    src_rows, tap_rows, rcv_rows = response.shape
    tile_time = direct_wave.shape[1]
    groups, src_n, tim_n = (lax.axis_size(a) for a in ("grp", "src", "tim"))
    g, s, r, c = (lax.axis_index(a) for a in ("grp", "src", "rcv", "tim"))
    time = src_n * tile_time
    rows = src_rows // groups
    part_time = tile_time // tim_n
    pos = jnp.stack([g * rows, c * tap_rows]).astype(jnp.int32)

    direct_piece = lax.dynamic_slice_in_dim(direct_wave, c * part_time, part_time, 1).T
    my_arrival = lax.dynamic_slice_in_dim(arrival, s * src_rows, src_rows).reshape(groups, rows)
    src_arrival = jnp.stack(total_order(scatter_parts(my_arrival, "grp"), "grp"))
    rcv_arrival = lax.dynamic_slice_in_dim(arrival, r * rcv_rows, rcv_rows)

    def whole_field(piece):
        field = gather(gather(gather(piece, "grp"), "src"), "tim")
        return field.transpose(2, 1, 0, 3, 4).reshape(groups * time, rcv_rows)

    current = whole_field(direct_piece)
    kept, energy = load_kept(pos, response, onset, rows)
    energy = jnp.broadcast_to(energy, (8, 128))
    for axis in ("tim", "rcv", "grp", "src"):
        energy = jnp.sum(gather(energy, axis), axis=0)
    unit_gain = lax.rsqrt(energy[0, 0] / STATIONS + 1e-06)

    halves = 2 if rows % 32 == 0 and rows >= 64 else 1
    half = rows // halves
    share = half // tim_n
    up_time = lax.broadcasted_iota(jnp.int32, (1, 1, time), 2)
    piece_time = s * tile_time + c * part_time
    piece_time = piece_time + lax.broadcasted_iota(jnp.int32, (part_time, 1), 0)

    focus_up = piece = None
    for iteration in range(ITERS):
        final_pass = iteration + 1 == ITERS
        ups, outs = [], []
        for h in range(halves):
            partial = forward(pos, kept, current, h * half, half, groups)
            partial = partial.astype(bf16).reshape(tim_n, share, groups * time)
            mine = total_of(scatter_parts(partial, "tim")).astype(bf16)
            total = jnp.sum(gather(mine, "rcv").astype(f32), axis=0)
            total = total.reshape(share, groups, time)
            limit = lax.dynamic_slice_in_dim(src_arrival, h * half + c * share, share, 1)
            inside = up_time < limit.T[:, :, None]
            up = jnp.where(inside, total, 0.0).reshape(share, groups * time)
            ups.append(gather(up.astype(bf16), "tim").reshape(half, groups * time))
            if final_pass:
                scaled = jnp.where(inside, unit_gain * total, 0.0).astype(bf16)
                outs.append(gather(scaled, "tim").reshape(half, groups, time))
        acc = None
        for h in range(halves):
            kind = bf16 if h + 1 == halves else f32
            acc = backward(pos, kept, ups[h], acc, h * half, groups, kind)
        sums = acc.reshape(groups, src_n, tim_n, part_time, rcv_rows)
        sums = total_of(scatter_parts(sums.transpose(2, 0, 1, 3, 4), "tim")).astype(bf16)
        sums = total_of(scatter_parts(sums, "grp")).astype(bf16)
        sums = total_of(scatter_parts(sums, "src"))
        piece = (
            direct_piece.astype(f32)
            + jnp.where(piece_time < rcv_arrival[None, :], unit_gain * unit_gain * sums, 0.0)
        ).astype(bf16)
        if final_pass:
            out = jnp.concatenate(outs).transpose(1, 0, 2)
            focus_up = jnp.concatenate(total_order(scatter_parts(out, "grp"), "grp"))
            focus_down = gather(piece, "tim").reshape(tile_time, rcv_rows).T
        else:
            current = whole_field(piece)
    return (focus_down, focus_up)


def total_order(parts, axis):
    n = lax.axis_size(axis)
    if n == 1 or n > 8:
        return parts
    stack = jnp.stack(parts)
    me = lax.axis_index(axis)
    return [lax.dynamic_index_in_dim(stack, (me - i) % n, 0, False) for i in range(n)]


def solution(mesh):
    in_specs = (P("src", "tim", "rcv"), P("src", "rcv"), P(("grp", "rcv"), "src"), P("grp"))
    out_specs = (P(("grp", "rcv"), "src"), P(("grp", "src"), None))
    return jax.shard_map(
        on_device, mesh=mesh, in_specs=in_specs, out_specs=out_specs, check_vma=False
    )
```

time: 831 us -> 308 us (0.37)
  local copies, waits for them, and re-layouts: 332 us -> 53.4 us
  matrix products: 208 us -> 0 us
  Pallas kernels: 0 us -> 139 us
  other arithmetic: 116 us -> 11 us
  blocking collectives: 77.6 us -> 0 us
  starting transfers between devices: 0.16 us -> 39.2 us
  waiting for transfers between devices: 79.4 us -> 58.7 us
  between operations: 14.6 us -> 2.51 us
    dot_general x4 -> x0, matrix products: 208 us -> none  [the longest x2 146 us: on_device(): lax.dot_general(kept_resp, current, (((2,), (0,)), ((), ())), preferred_e...]
    pallas_call x0 -> x9, Pallas kernels: none -> 139 us  [the longest x4 70.2 us: backward(): pl.pallas_call(functools.partial(backward_kernel, first=first, groups=gro...]
    reshape x4 -> x1, local copies, waits for them, and re-layouts: 124 us -> 0.02 us  [on_device(): lax.dynamic_slice_in_dim(arrival, s * src_rows, src_rows)]
    slice x6 -> x1, local copies, waits for them, and re-layouts: 84.3 us -> 0.51 us  [on_device(): unit_gain = lax.rsqrt(energy[0, 0] / STATIONS + 1e-06)]
    pad x4 -> x0, local copies, waits for them, and re-layouts: 68.6 us -> none  [the longest x2 52.2 us: delay_sum(): padded = jnp.pad(product, ((0, 0), (0, 0), (0, taps_here)))]
    reduce_sum x3 -> x8, other arithmetic: 67.3 us -> 0.3 us  [the longest x4 0.25 us: on_device(): total = jnp.sum(gather(mine, 'rcv').astype(f32), axis=0)]
    reduce_scatter x2 -> x0, waiting for transfers between devices: 61.5 us -> none  [on_device(): lax.psum_scatter(backward_sum, ('src', 'tim'), scatter_dimension=1, tiled...]
    ppermute x0 -> x43, waiting for transfers between devices: none -> 58.7 us  [shifted(): return lax.ppermute(x, axis, [(i, (i + shift) % n) for i in range(n)])]
  transfers between devices with their start and end apart: 4 -> 43, of which waited for: 3 -> 21; matrix products, arithmetic and copies ran while one was open for 5% -> 4% of each run, Pallas kernels for 0% -> 16%
where the time goes in v1:
time: 308 us; the launch traced here: 304 us
  Pallas kernels  139 us (45%)
  waiting for transfers between devices  58.7 us (19%)
  local copies, waits for them, and re-layouts  53.4 us (17%)
  starting transfers between devices  39.2 us (13%)
  other arithmetic  11 us (4%)
    pallas_call x4, Pallas kernels, backward(): pl.pallas_call(functools.partial(backward_kernel, first=first, groups=gro...  70.2 us
    ppermute x43, waiting for transfers between devices, shifted(): return lax.ppermute(x, axis, [(i, (i + shift) % n) for i in range(n)])  58.7 us
    pallas_call x4, Pallas kernels, forward(): pl.pallas_call(functools.partial(forward_kernel, first=first, groups=grou...  56.3 us
    unnamed x40, local copies, waits for them, and re-layouts  44.4 us
    ppermute x43, starting transfers between devices, shifted(): return lax.ppermute(x, axis, [(i, (i + shift) % n) for i in range(n)])  39.2 us
    pallas_call x1, Pallas kernels, load_kept(): pl.pallas_call(functools.partial(load_kernel, chunks=chunks, sub=sub), in...  12.5 us
  transfers between devices with their start and end apart: 43, of which 21 were waited for; matrix products, arithmetic and copies ran while one was open for 4% of the time, Pallas kernels for 16%

profile of v1, /device:TPU:0, one launch (start us, length us, event | category | flops | bytes accessed | tf_op | source)
XLA Modules:
  0.0 303.8 jit_solution(1957095779911500678)
XLA Ops:
  1.5 3.0 collective-permute-start.7
  6.8 4.2 %collective-permute-start.8 = (bf16[2,32,1024]{2,1,0:T(8,128)(2,1)S(1)}, bf16[2,32,1024]{2,1,0:T(8,128)(2,1)S(1)}, u32[]{:S(2)}, u32[]{:S(2)}) collective-permute-start(bf16[2,32,1024]{2,1,0:T(8,128)(2,1)S(1)} %get-tuple-element.17), channel_id=1, source_target_pairs={{0,12},{4,0},{8,4},{12,8},{1,13},{5,1},{9,5},{13,9},{2,14},{6,2},{... | collective-permute-start | bytes 393224 | tf_op jit(solution)/shard_map/ppermute | solution.py:189
  14.2 12.5 %load_kept.1 = (bf16[256,64,1024]{2,1,0:T(8,128)(2,1)S(1)}, f32[1]{0:T(128)}) custom-call(s32[2]{0:T(128)S(1)} %pad_add_fusion.pos_ref, bf16[512,64,1024]{2,1,0:T(8,128)(2,1)} %r_hbm.1, s32[512,1024]{1,0:T(8,128)S(1)} %copy-done.4), custom_call_target="tpu_custom_call" | custom-call | bytes 33554432 | tf_op jit(solution)/shard_map/load_kept/pallas_call | solution.py:59
  26.7 11.1 %copy-done = bf16[256,64,1024]{2,1,0:T(8,128)(2,1)} copy-done((bf16[256,64,1024]{2,1,0:T(8,128)(2,1)}, bf16[256,64,1024]{2,1,0:T(8,128)(2,1)S(1)}, u32[]{:S(2)}) %copy-start) | copy-done | bytes 33554456
  40.1 8.7 %collective-permute-done.9 = bf16[2,32,1024]{2,1,0:T(8,128)(2,1)S(1)} collective-permute-done((bf16[2,32,1024]{2,1,0:T(8,128)(2,1)S(1)}, bf16[2,32,1024]{2,1,0:T(8,128)(2,1)S(1)}, u32[]{:S(2)}, u32[]{:S(2)}) %collective-permute-start.9) | collective-permute-done | bytes 131104 | tf_op jit(solution)/shard_map/ppermute | solution.py:189
  54.9 2.4 collective-permute-done.2
  59.0 10.5 %copy-done.1 = bf16[256,64,1024]{2,1,0:T(8,128)(2,1)S(1)} copy-done((bf16[256,64,1024]{2,1,0:T(8,128)(2,1)S(1)}, bf16[256,64,1024]{2,1,0:T(8,128)(2,1)}, u32[]{:S(2)}) %copy-start.1) | copy-done | bytes 33554456
  69.6 14.1 %forward.5 = f32[128,512]{1,0:T(8,128)} custom-call(s32[2]{0:T(128)} %copy-done.5, bf16[256,64,1024]{2,1,0:T(8,128)(2,1)S(1)} %copy-done.1, bf16[512,1024]{1,0:T(8,128)(2,1)} %bitcast.193), custom_call_target="tpu_custom_call" | custom-call | flops 8589934592 | bytes 1048576 | tf_op jit(solution)/shard_map/forward/pallas_call | solution.py:119
  83.6 14.1 %forward.4 = f32[128,512]{1,0:T(8,128)} custom-call(s32[2]{0:T(128)} %copy-done.5, bf16[256,64,1024]{2,1,0:T(8,128)(2,1)S(1)} %copy-done.1, bf16[512,1024]{1,0:T(8,128)(2,1)} %bitcast.194), custom_call_target="tpu_custom_call" | custom-call | flops 8589934592 | bytes 1048576 | tf_op jit(solution)/shard_map/forward/pallas_call | solution.py:119
  103.6 2.2 collective-permute-start.5
  108.2 17.3 %backward.4.refs_0_ = f32[512,1024]{1,0:T(8,128)} custom-call(s32[2]{0:T(128)} %copy-done.5, bf16[256,64,1024]{2,1,0:T(8,128)(2,1)S(1)} %copy-done.1, bf16[128,512]{1,0:T(8,128)(2,1)} %bitcast.206), custom_call_target="tpu_custom_call" | custom-call | flops 8589934592 | bytes 2097152 | tf_op jit(solution)/shard_map/backward/pallas_call | solution.py:173
  126.2 17.7 %backward.5 = bf16[512,1024]{1,0:T(8,128)(2,1)} custom-call(s32[2]{0:T(128)} %copy-done.5, bf16[256,64,1024]{2,1,0:T(8,128)(2,1)S(1)} %copy-done.1, bf16[128,512]{1,0:T(8,128)(2,1)} %bitcast.205, f32[512,1024]{1,0:T(8,128)} %backward.4.refs_0_), custom_call_target="tpu_custom_call" | custom-call | flops 8589934592 | bytes 2097152 | tf_op jit(solution)/shard_map/backward/pallas_call | solution.py:173
  148.8 8.1 %collective-permute-done.19 = bf16[4,32,1024]{2,1,0:T(8,128)(2,1)S(1)} collective-permute-done((bf16[4,32,1024]{2,1,0:T(8,128)(2,1)S(1)}, bf16[4,32,1024]{2,1,0:T(8,128)(2,1)S(1)}, u32[]{:S(2)}, u32[]{:S(2)}) %collective-permute-start.19) | collective-permute-done | bytes 262176 | tf_op jit(solution)/shard_map/ppermute | solution.py:189
  161.5 4.1 %collective-permute-done.21 = bf16[32,1024]{1,0:T(8,128)(2,1)S(1)} collective-permute-done((bf16[32,1024]{1,0:T(8,128)(2,1)S(1)}, bf16[32,1024]{1,0:T(8,128)(2,1)S(1)}, u32[]{:S(2)}, u32[]{:S(2)}) %collective-permute-start.21) | collective-permute-done | bytes 65568 | tf_op jit(solution)/shard_map/ppermute | solution.py:189
  166.3 3.8 %collective-permute-done.23 = bf16[32,1024]{1,0:T(8,128)(2,1)S(1)} collective-permute-done((bf16[32,1024]{1,0:T(8,128)(2,1)S(1)}, bf16[32,1024]{1,0:T(8,128)(2,1)S(1)}, u32[]{:S(2)}, u32[]{:S(2)}) %collective-permute-start.23) | collective-permute-done | bytes 65568 | tf_op jit(solution)/shard_map/ppermute | solution.py:189
  175.3 7.1 %collective-permute-done.25 = bf16[2,32,1024]{2,1,0:T(8,128)(2,1)S(1)} collective-permute-done((bf16[2,32,1024]{2,1,0:T(8,128)(2,1)S(1)}, bf16[2,32,1024]{2,1,0:T(8,128)(2,1)S(1)}, u32[]{:S(2)}, u32[]{:S(2)}) %collective-permute-start.25) | collective-permute-done | bytes 131104 | tf_op jit(solution)/shard_map/ppermute | solution.py:189
  186.1 10.5 %copy-done.2 = bf16[256,64,1024]{2,1,0:T(8,128)(2,1)S(1)} copy-done((bf16[256,64,1024]{2,1,0:T(8,128)(2,1)S(1)}, bf16[256,64,1024]{2,1,0:T(8,128)(2,1)}, u32[]{:S(2)}) %copy-start.2) | copy-done | bytes 33554456
  196.6 14.1 %forward.7 = f32[128,512]{1,0:T(8,128)} custom-call(s32[2]{0:T(128)} %copy-done.5, bf16[256,64,1024]{2,1,0:T(8,128)(2,1)S(1)} %copy-done.2, bf16[512,1024]{1,0:T(8,128)(2,1)} %bitcast.195), custom_call_target="tpu_custom_call" | custom-call | flops 8589934592 | bytes 1048576 | tf_op jit(solution)/shard_map/forward/pallas_call | solution.py:119
  210.7 14.1 %forward.6 = f32[128,512]{1,0:T(8,128)} custom-call(s32[2]{0:T(128)} %copy-done.5, bf16[256,64,1024]{2,1,0:T(8,128)(2,1)S(1)} %copy-done.2, bf16[512,1024]{1,0:T(8,128)(2,1)} %bitcast.196), custom_call_target="tpu_custom_call" | custom-call | flops 8589934592 | bytes 1048576 | tf_op jit(solution)/shard_map/forward/pallas_call | solution.py:119
  235.0 10.5 %copy-done.3 = bf16[256,64,1024]{2,1,0:T(8,128)(2,1)S(1)} copy-done((bf16[256,64,1024]{2,1,0:T(8,128)(2,1)S(1)}, bf16[256,64,1024]{2,1,0:T(8,128)(2,1)}, u32[]{:S(2)}) %copy-start.3) | copy-done | bytes 33554456
  245.6 17.3 %backward.6.refs_0_ = f32[512,1024]{1,0:T(8,128)} custom-call(s32[2]{0:T(128)} %copy-done.5, bf16[256,64,1024]{2,1,0:T(8,128)(2,1)S(1)} %copy-done.3, bf16[128,512]{1,0:T(8,128)(2,1)} %bitcast.204), custom_call_target="tpu_custom_call" | custom-call | flops 8589934592 | bytes 2097152 | tf_op jit(solution)/shard_map/backward/pallas_call | solution.py:173
  262.9 17.9 %backward.7 = bf16[512,1024]{1,0:T(8,128)(2,1)} custom-call(s32[2]{0:T(128)} %copy-done.5, bf16[256,64,1024]{2,1,0:T(8,128)(2,1)S(1)} %copy-done.3, bf16[128,512]{1,0:T(8,128)(2,1)} %bitcast.203, f32[512,1024]{1,0:T(8,128)} %backward.6.refs_0_), custom_call_target="tpu_custom_call" | custom-call | flops 8589934592 | bytes 2097152 | tf_op jit(solution)/shard_map/backward/pallas_call | solution.py:173
  287.5 5.9 %collective-permute-done.35 = bf16[4,32,1024]{2,1,0:T(8,128)(2,1)S(1)} collective-permute-done((bf16[4,32,1024]{2,1,0:T(8,128)(2,1)S(1)}, bf16[4,32,1024]{2,1,0:T(8,128)(2,1)S(1)}, u32[]{:S(2)}, u32[]{:S(2)}) %collective-permute-start.35) | collective-permute-done | bytes 262176 | tf_op jit(solution)/shard_map/ppermute | solution.py:189
  297.9 2.5 collective-permute-done.37
  (198 shorter events, 67.8 us)
Async XLA Ops:
  1.5 5.3 %collective-permute-start.7 = (bf16[32,1024]{1,0:T(8,128)(2,1)S(1)}, bf16[32,1024]{1,0:T(8,128)(2,1)S(1)}, u32[]{:S(2)}, u32[]{:S(2)}) collective-permute-start(bf16[32,1024]{1,0:T(8,128)(2,1)S(1)} %get-tuple-element.33), channel_id=1, source_target_pairs={{0,16},{16,0},{1,17},{17,1},{2,18},{18,2},{3,19},{19,3},{4,20},{20... | collective-permute-start | bytes 196616 | tf_op jit(solution)/shard_map/ppermute | solution.py:189
  6.8 33.3 %collective-permute-start.8 = (bf16[2,32,1024]{2,1,0:T(8,128)(2,1)S(1)}, bf16[2,32,1024]{2,1,0:T(8,128)(2,1)S(1)}, u32[]{:S(2)}, u32[]{:S(2)}) collective-permute-start(bf16[2,32,1024]{2,1,0:T(8,128)(2,1)S(1)} %get-tuple-element.17), channel_id=1, source_target_pairs={{0,12},{4,0},{8,4},{12,8},{1,13},{5,1},{9,5},{13,9},{2,14},{6,2},{... | collective-permute-start | bytes 393224 | tf_op jit(solution)/shard_map/ppermute | solution.py:189
  11.0 40.5 %collective-permute-start.6 = (s32[256]{0:T(256)S(1)}, s32[256]{0:T(256)S(1)}, u32[]{:S(2)}, u32[]{:S(2)}) collective-permute-start(s32[256]{0:T(256)S(1)} %bitcast.250), channel_id=1, source_target_pairs={{0,16},{16,0},{1,17},{17,1},{2,18},{18,2},{3,19},{19,3},{4,20},{20... | collective-permute-start | bytes 3080 | tf_op jit(solution)/shard_map/ppermute | solution.py:189
  38.4 10.8 %collective-permute-start = (f32[8,128]{1,0:T(8,128)S(1)}, f32[8,128]{1,0:T(8,128)S(1)}, u32[]{:S(2)}, u32[]{:S(2)}) collective-permute-start(f32[8,128]{1,0:T(8,128)S(1)} %broadcast_in_dim.31), channel_id=1, source_target_pairs={{0,1},{1,0},{2,3},{3,2},{4,5},{5,4},{6,7},{7,6},{8,9},{9,8},{10,11... | collective-permute-start | bytes 12296 | tf_op jit(solution)/shard_map/ppermute | solution.py:189
  38.5 10.3 %collective-permute-start.9 = (bf16[2,32,1024]{2,1,0:T(8,128)(2,1)S(1)}, bf16[2,32,1024]{2,1,0:T(8,128)(2,1)S(1)}, u32[]{:S(2)}, u32[]{:S(2)}) collective-permute-start(bf16[2,32,1024]{2,1,0:T(8,128)(2,1)S(1)} %get-tuple-element.17), channel_id=1, source_target_pairs={{0,8},{4,12},{8,0},{12,4},{1,9},{5,13},{9,1},{13,5},{2,10},{6,14},... | collective-permute-start | bytes 393224 | tf_op jit(solution)/shard_map/ppermute | solution.py:189
  38.6 10.2 %collective-permute-start.10 = (bf16[2,32,1024]{2,1,0:T(8,128)(2,1)S(1)}, bf16[2,32,1024]{2,1,0:T(8,128)(2,1)S(1)}, u32[]{:S(2)}, u32[]{:S(2)}) collective-permute-start(bf16[2,32,1024]{2,1,0:T(8,128)(2,1)S(1)} %get-tuple-element.17), channel_id=1, source_target_pairs={{0,4},{4,8},{8,12},{12,0},{1,5},{5,9},{9,13},{13,1},{2,6},{6,10},{... | collective-permute-start | bytes 393224 | tf_op jit(solution)/shard_map/ppermute | solution.py:189
  48.9 8.4 %collective-permute-start.11 = (bf16[4,2,32,1024]{3,2,1,0:T(8,128)(2,1)S(1)}, bf16[4,2,32,1024]{3,2,1,0:T(8,128)(2,1)S(1)}, u32[]{:S(2)}, u32[]{:S(2)}) collective-permute-start(bf16[4,2,32,1024]{3,2,1,0:T(8,128)(2,1)S(1)} %constant_dynamic-slice_fusion.12), channel_id=1, source_target_pairs={{0,1},{1,0},{2,3},{3,2},{4,5},{5,4},{6,7},{7,6},{8,9},{9,8},{10,11... | collective-permute-start | bytes 1572872 | tf_op jit(solution)/shard_map/ppermute | solution.py:189
  99.4 6.3 %collective-permute-start.16 = (bf16[64,512]{1,0:T(8,128)(2,1)S(1)}, bf16[64,512]{1,0:T(8,128)(2,1)S(1)}, u32[]{:S(2)}, u32[]{:S(2)}) collective-permute-start(bf16[64,512]{1,0:T(8,128)(2,1)S(1)} %fusion.58), channel_id=1, source_target_pairs={{0,2},{2,0},{1,3},{3,1},{4,6},{6,4},{5,7},{7,5},{8,10},{10,8},{9,1... | collective-permute-start | bytes 196616 | tf_op jit(solution)/shard_map/ppermute | solution.py:189
  101.0 4.8 %collective-permute-start.13 = (bf16[64,512]{1,0:T(8,128)(2,1)S(1)}, bf16[64,512]{1,0:T(8,128)(2,1)S(1)}, u32[]{:S(2)}, u32[]{:S(2)}) collective-permute-start(bf16[64,512]{1,0:T(8,128)(2,1)S(1)} %fusion.59), channel_id=1, source_target_pairs={{0,2},{2,0},{1,3},{3,1},{4,6},{6,4},{5,7},{7,5},{8,10},{10,8},{9,1... | collective-permute-start | bytes 196616 | tf_op jit(solution)/shard_map/ppermute | solution.py:189
  101.9 43.6 %collective-permute-start.3 = (f32[8,128]{1,0:T(8,128)S(1)}, f32[8,128]{1,0:T(8,128)S(1)}, u32[]{:S(2)}, u32[]{:S(2)}) collective-permute-start(f32[8,128]{1,0:T(8,128)S(1)} %fusion.70), channel_id=1, source_target_pairs={{0,12},{4,0},{8,4},{12,8},{1,13},{5,1},{9,5},{13,9},{2,14},{6,2},{... | collective-permute-start | bytes 12296 | tf_op jit(solution)/shard_map/ppermute | solution.py:189
  102.3 43.1 %collective-permute-start.4 = (f32[8,128]{1,0:T(8,128)S(1)}, f32[8,128]{1,0:T(8,128)S(1)}, u32[]{:S(2)}, u32[]{:S(2)}) collective-permute-start(f32[8,128]{1,0:T(8,128)S(1)} %fusion.70), channel_id=1, source_target_pairs={{0,8},{4,12},{8,0},{12,4},{1,9},{5,13},{9,1},{13,5},{2,10},{6,14},... | collective-permute-start | bytes 12296 | tf_op jit(solution)/shard_map/ppermute | solution.py:189
  103.6 41.9 %collective-permute-start.5 = (f32[8,128]{1,0:T(8,128)S(1)}, f32[8,128]{1,0:T(8,128)S(1)}, u32[]{:S(2)}, u32[]{:S(2)}) collective-permute-start(f32[8,128]{1,0:T(8,128)S(1)} %fusion.70), channel_id=1, source_target_pairs={{0,4},{4,8},{8,12},{12,0},{1,5},{5,9},{9,13},{13,1},{2,6},{6,10},{... | collective-permute-start | bytes 12296 | tf_op jit(solution)/shard_map/ppermute | solution.py:189
  106.0 19.5 %collective-permute-start.14 = (bf16[64,512]{1,0:T(8,128)(2,1)S(1)}, bf16[64,512]{1,0:T(8,128)(2,1)S(1)}, u32[]{:S(2)}, u32[]{:S(2)}) collective-permute-start(bf16[64,512]{1,0:T(8,128)(2,1)S(1)} %get-tuple-element.34), channel_id=1, source_target_pairs={{0,1},{1,0},{2,3},{3,2},{4,5},{5,4},{6,7},{7,6},{8,9},{9,8},{10,11... | collective-permute-start | bytes 196616 | tf_op jit(solution)/shard_map/ppermute | solution.py:189
  148.3 8.6 %collective-permute-start.19 = (bf16[4,32,1024]{2,1,0:T(8,128)(2,1)S(1)}, bf16[4,32,1024]{2,1,0:T(8,128)(2,1)S(1)}, u32[]{:S(2)}, u32[]{:S(2)}) collective-permute-start(bf16[4,32,1024]{2,1,0:T(8,128)(2,1)S(1)} %dynamic-slice_bitcast_fusion.3), channel_id=1, source_target_pairs={{0,16},{16,0},{1,17},{17,1},{2,18},{18,2},{3,19},{19,3},{4,20},{20... | collective-permute-start | bytes 786440 | tf_op jit(solution)/shard_map/ppermute | solution.py:189
  157.0 4.5 %collective-permute-start.22 = (bf16[32,1024]{1,0:T(8,128)(2,1)S(1)}, bf16[32,1024]{1,0:T(8,128)(2,1)S(1)}, u32[]{:S(2)}, u32[]{:S(2)}) collective-permute-start(bf16[32,1024]{1,0:T(8,128)(2,1)S(1)} %get-tuple-element.26), channel_id=1, source_target_pairs={{0,12},{4,0},{8,4},{12,8},{1,13},{5,1},{9,5},{13,9},{2,14},{6,2},{... | collective-permute-start | bytes 196616 | tf_op jit(solution)/shard_map/ppermute | solution.py:189
  158.9 6.8 %collective-permute-start.21 = (bf16[32,1024]{1,0:T(8,128)(2,1)S(1)}, bf16[32,1024]{1,0:T(8,128)(2,1)S(1)}, u32[]{:S(2)}, u32[]{:S(2)}) collective-permute-start(bf16[32,1024]{1,0:T(8,128)(2,1)S(1)} %get-tuple-element.27), channel_id=1, source_target_pairs={{0,8},{4,12},{8,0},{12,4},{1,9},{5,13},{9,1},{13,5},{2,10},{6,14},... | collective-permute-start | bytes 196616 | tf_op jit(solution)/shard_map/ppermute | solution.py:189
  158.9 6.8 %collective-permute-start.20 = (bf16[32,1024]{1,0:T(8,128)(2,1)S(1)}, bf16[32,1024]{1,0:T(8,128)(2,1)S(1)}, u32[]{:S(2)}, u32[]{:S(2)}) collective-permute-start(bf16[32,1024]{1,0:T(8,128)(2,1)S(1)} %get-tuple-element.25), channel_id=1, source_target_pairs={{0,4},{4,8},{8,12},{12,0},{1,5},{5,9},{9,13},{13,1},{2,6},{6,10},{... | collective-permute-start | bytes 196616 | tf_op jit(solution)/shard_map/ppermute | solution.py:189
  170.2 5.1 %collective-permute-start.24 = (bf16[2,32,1024]{2,1,0:T(8,128)(2,1)S(1)}, bf16[2,32,1024]{2,1,0:T(8,128)(2,1)S(1)}, u32[]{:S(2)}, u32[]{:S(2)}) collective-permute-start(bf16[2,32,1024]{2,1,0:T(8,128)(2,1)S(1)} %get-tuple-element.7), channel_id=1, source_target_pairs={{0,12},{4,0},{8,4},{12,8},{1,13},{5,1},{9,5},{13,9},{2,14},{6,2},{... | collective-permute-start | bytes 393224 | tf_op jit(solution)/shard_map/ppermute | solution.py:189
  171.7 10.6 %collective-permute-start.25 = (bf16[2,32,1024]{2,1,0:T(8,128)(2,1)S(1)}, bf16[2,32,1024]{2,1,0:T(8,128)(2,1)S(1)}, u32[]{:S(2)}, u32[]{:S(2)}) collective-permute-start(bf16[2,32,1024]{2,1,0:T(8,128)(2,1)S(1)} %get-tuple-element.7), channel_id=1, source_target_pairs={{0,8},{4,12},{8,0},{12,4},{1,9},{5,13},{9,1},{13,5},{2,10},{6,14},... | collective-permute-start | bytes 393224 | tf_op jit(solution)/shard_map/ppermute | solution.py:189
  171.8 10.5 %collective-permute-start.26 = (bf16[2,32,1024]{2,1,0:T(8,128)(2,1)S(1)}, bf16[2,32,1024]{2,1,0:T(8,128)(2,1)S(1)}, u32[]{:S(2)}, u32[]{:S(2)}) collective-permute-start(bf16[2,32,1024]{2,1,0:T(8,128)(2,1)S(1)} %get-tuple-element.7), channel_id=1, source_target_pairs={{0,4},{4,8},{8,12},{12,0},{1,5},{5,9},{9,13},{13,1},{2,6},{6,10},{... | collective-permute-start | bytes 393224 | tf_op jit(solution)/shard_map/ppermute | solution.py:189
  284.2 9.2 %collective-permute-start.35 = (bf16[4,32,1024]{2,1,0:T(8,128)(2,1)S(1)}, bf16[4,32,1024]{2,1,0:T(8,128)(2,1)S(1)}, u32[]{:S(2)}, u32[]{:S(2)}) collective-permute-start(bf16[4,32,1024]{2,1,0:T(8,128)(2,1)S(1)} %dynamic-slice_bitcast_fusion.2), channel_id=1, source_target_pairs={{0,16},{16,0},{1,17},{17,1},{2,18},{18,2},{3,19},{19,3},{4,20},{20... | collective-permute-start | bytes 786440 | tf_op jit(solution)/shard_map/ppermute | solution.py:189
  285.9 11.4 %collective-permute-start.42 = (bf16[256,256]{1,0:T(8,128)(2,1)S(1)}, bf16[256,256]{1,0:T(8,128)(2,1)S(1)}, u32[]{:S(2)}, u32[]{:S(2)}) collective-permute-start(bf16[256,256]{1,0:T(8,128)(2,1)S(1)} %get-tuple-element.20), channel_id=1, source_target_pairs={{0,16},{16,0},{1,17},{17,1},{2,18},{18,2},{3,19},{19,3},{4,20},{20... | collective-permute-start | bytes 393224 | tf_op jit(solution)/shard_map/ppermute | solution.py:189
  293.7 6.6 %collective-permute-start.37 = (bf16[32,1024]{1,0:T(8,128)(2,1)S(1)}, bf16[32,1024]{1,0:T(8,128)(2,1)S(1)}, u32[]{:S(2)}, u32[]{:S(2)}) collective-permute-start(bf16[32,1024]{1,0:T(8,128)(2,1)S(1)} %get-tuple-element.24), channel_id=1, source_target_pairs={{0,8},{4,12},{8,0},{12,4},{1,9},{5,13},{9,1},{13,5},{2,10},{6,14},... | collective-permute-start | bytes 196616 | tf_op jit(solution)/shard_map/ppermute | solution.py:189
  295.3 6.1 %collective-permute-start.36 = (bf16[32,1024]{1,0:T(8,128)(2,1)S(1)}, bf16[32,1024]{1,0:T(8,128)(2,1)S(1)}, u32[]{:S(2)}, u32[]{:S(2)}) collective-permute-start(bf16[32,1024]{1,0:T(8,128)(2,1)S(1)} %get-tuple-element.22), channel_id=1, source_target_pairs={{0,4},{4,8},{8,12},{12,0},{1,5},{5,9},{9,13},{13,1},{2,6},{6,10},{... | collective-permute-start | bytes 196616 | tf_op jit(solution)/shard_map/ppermute | solution.py:189
  (29 other events, 148.5 us)

commit v2 on v1

v2 whole, which is shorter than its diff:
```python
import functools

import jax
import jax.numpy as jnp
from jax import lax
from jax.experimental import pallas as pl
from jax.experimental.pallas import tpu as pltpu
from jax.sharding import PartitionSpec as P

STATIONS = 2048
ITERS = 2
MIB = 1 << 20
bf16 = jnp.bfloat16
f32 = jnp.float32
VM = pl.BlockSpec(memory_space=pltpu.VMEM)
SM = pl.BlockSpec(memory_space=pltpu.SMEM)
ANY = pl.BlockSpec(memory_space=pl.ANY)


class Stream:
    def __init__(self, k_hbm, ring, sem, size):
        self.k_hbm, self.ring, self.sem, self.size = k_hbm, ring, sem, size
        self.slots, self.count = ring.shape[0], k_hbm.shape[0] // size

    def copy(self, step):
        slot = lax.rem(step, self.slots)
        return pltpu.make_async_copy(
            self.k_hbm.at[pl.ds(step * self.size, self.size)], self.ring.at[slot], self.sem.at[slot]
        )

    def start(self):
        for c in range(min(self.slots - 1, self.count)):
            self.copy(jnp.int32(c)).start()

    def next(self, step):
        self.copy(step).wait()

        @pl.when(step + self.slots - 1 < self.count)
        def _():
            self.copy(step + self.slots - 1).start()

        return lax.rem(step, self.slots)


def ring_of(rows, taps, cols):
    sub, unroll = steps_of(rows)
    return [pltpu.VMEM((3, sub * unroll, taps, cols), bf16), pltpu.SemaphoreType.DMA((3,))]


def steps_of(rows):
    sub = min(16, rows)
    unroll = 2 if rows % (2 * sub) == 0 else 1
    return sub, unroll


def place_blocks(where_ref, blocks, f_ref):
    many, size = blocks[0].shape[0], blocks[0].shape[1]
    for b, block in enumerate(blocks):
        for i in range(many):
            to = where_ref[b * many + i]
            f_ref[pl.ds(pl.multiple_of(to, size), size)] = block[i]


def shear_sum(k, f_ref, tap_start, groups, put):
    sub, taps, cols = k.shape
    time = f_ref.shape[0] // groups
    sample = lax.broadcasted_iota(jnp.int32, (8, time), 0) + lax.broadcasted_iota(
        jnp.int32, (8, time), 1
    )
    p = lax.dot_general(
        k.reshape(sub * taps, cols),
        f_ref[...],
        (((1,), (1,)), ((), ())),
        preferred_element_type=f32,
    )
    p = p.reshape(sub, taps // 8, 8, groups * time)
    for g in range(groups):
        total = None
        for j in range(taps // 8 - 1, -1, -1):
            inside = (sample < time - tap_start - 8 * j)[None]
            term = jnp.where(inside, p[:, j, :, g * time : (g + 1) * time], 0.0)
            total = term if total is None else pltpu.roll(total, 8, 2) + term
        total = pltpu.roll(total, 0, 2, stride=1, stride_axis=1)
        put(g * time, (g + 1) * time, pltpu.roll(jnp.sum(total, axis=1), tap_start, 1))


def forward_kernel(pos_ref, where_ref, k_hbm, *refs, groups, waits):
    blocks, (o_ref, f_ref, ring, sem) = refs[waits:-4], refs[-4:]
    rows, taps, cols = k_hbm.shape
    sub, unroll = steps_of(rows)
    stream = Stream(k_hbm, ring, sem, sub * unroll)
    stream.start()
    tap_start = pos_ref[1]
    place_blocks(where_ref, blocks, f_ref)

    def body(step, carry):
        slot = stream.next(step)
        for u in range(unroll):
            at = pl.multiple_of((step * unroll + u) * sub, sub)

            def put(lo, hi, value):
                o_ref[pl.ds(at, sub), lo:hi] = value

            k = ring[slot, u * sub : (u + 1) * sub]
            shear_sum(k, f_ref, tap_start, groups, put)
        return carry

    lax.fori_loop(0, rows // (sub * unroll), body, 0)


def first_kernel(pos_ref, where_ref, r_hbm, on_hbm, *refs, groups, waits):
    blocks, refs = refs[waits:-10], refs[-10:]
    o_ref, k_hbm, e_out, f_ref, ring, sem, out_sem, on_ref, e_ref, on_sem = refs
    rows, taps, cols = k_hbm.shape
    sub, unroll = steps_of(rows)
    size, slots = sub * unroll, ring.shape[0]
    count = rows // size
    ahead = slots - 2
    start = pl.multiple_of(pos_ref[0], 8)
    tap_start = pos_ref[1]

    def part(step):
        slot = lax.rem(step, slots)
        return pltpu.make_async_copy(
            r_hbm.at[pl.ds(start + step * size, size)], ring.at[slot], sem.at[slot]
        )

    def result(step):
        slot = lax.rem(step, slots)
        return pltpu.make_async_copy(
            ring.at[slot], k_hbm.at[pl.ds(step * size, size)], out_sem.at[slot]
        )

    onset_copy = pltpu.make_async_copy(on_hbm.at[pl.ds(start, rows)], on_ref, on_sem)
    onset_copy.start()
    for n in range(min(ahead, count)):
        part(jnp.int32(n)).start()
    e_ref[...] = jnp.zeros_like(e_ref)
    tap = lax.broadcasted_iota(jnp.int32, (1, taps, 1), 1).astype(f32).astype(bf16)
    place_blocks(where_ref, blocks, f_ref)
    onset_copy.wait()

    def body(step, carry):
        slot = lax.rem(step, slots)
        part(step).wait()

        @pl.when(step + ahead < count)
        def _():
            @pl.when(step >= slots - ahead)
            def _():
                result(step - (slots - ahead)).wait()

            part(step + ahead).start()

        for u in range(unroll):
            at = pl.multiple_of((step * unroll + u) * sub, sub)

            def put(lo, hi, value):
                o_ref[pl.ds(at, sub), lo:hi] = value

            for v in range(0, sub, 8):
                r = ring[slot, u * sub + v : u * sub + v + 8]
                x = r.astype(f32)
                e_ref[...] += jnp.sum((x * x).reshape(taps, 8, cols), axis=0)
                on = (on_ref[pl.ds(at + v, 8)] - tap_start).astype(f32).astype(bf16)
                keep = jnp.broadcast_to(tap, r.shape) >= on[:, None, :]
                ring[slot, u * sub + v : u * sub + v + 8] = jnp.where(keep, r, jnp.zeros((), bf16))
            k = ring[slot, u * sub : (u + 1) * sub]
            shear_sum(k, f_ref, tap_start, groups, put)
        result(step).start()
        return carry

    lax.fori_loop(0, count, body, 0)
    for n in range(max(0, count - slots), count):
        result(jnp.int32(n)).wait()
    e_out[0] = jnp.sum(e_ref[...])


def first_forward(pos, where, response, onset, blocks, rows, width, after):
    _, taps, cols = response.shape
    groups = lax.axis_size("grp")
    sub, unroll = steps_of(rows)
    slots = 4
    return pl.pallas_call(
        functools.partial(first_kernel, groups=groups, waits=len(after)),
        in_specs=[SM, SM, ANY, ANY] + [ANY] * len(after) + [VM] * len(blocks),
        out_specs=[VM, ANY, SM],
        out_shape=[
            jax.ShapeDtypeStruct((rows, width), f32),
            pltpu.HBM((rows, taps, cols), bf16),
            jax.ShapeDtypeStruct((1,), f32),
        ],
        scratch_shapes=[
            pltpu.VMEM((width, cols), bf16),
            pltpu.VMEM((slots, sub * unroll, taps, cols), bf16),
            pltpu.SemaphoreType.DMA((slots,)),
            pltpu.SemaphoreType.DMA((slots,)),
            pltpu.VMEM((rows, cols), jnp.int32),
            pltpu.VMEM((8, cols), f32),
            pltpu.SemaphoreType.DMA,
        ],
        compiler_params=pltpu.CompilerParams(vmem_limit_bytes=44 * MIB),
        cost_estimate=pl.CostEstimate(
            flops=2 * rows * taps * cols * width, bytes_accessed=width * cols * 2, transcendentals=0
        ),
        name="first_forward",
    )(pos, where, response, onset, *after, *blocks)


def forward(pos, where, kept, blocks, width, after):
    rows, taps, cols = kept.shape
    groups = lax.axis_size("grp")
    return pl.pallas_call(
        functools.partial(forward_kernel, groups=groups, waits=len(after)),
        in_specs=[SM, SM, ANY] + [ANY] * len(after) + [VM] * len(blocks),
        out_specs=VM,
        out_shape=jax.ShapeDtypeStruct((rows, width), f32),
        scratch_shapes=[pltpu.VMEM((width, cols), bf16)] + ring_of(rows, taps, cols),
        compiler_params=pltpu.CompilerParams(vmem_limit_bytes=40 * MIB),
        cost_estimate=pl.CostEstimate(
            flops=2 * rows * taps * cols * width, bytes_accessed=width * cols * 2, transcendentals=0
        ),
        name="forward",
    )(pos, where, pltpu.with_memory_space_constraint(kept, pltpu.HBM), *after, *blocks)


def backward_kernel(pos_ref, k_hbm, u_ref, *refs, groups, waits):
    refs = refs[waits:]
    before_ref, (o_ref, acc_ref, ring, sem) = (refs[0] if len(refs) == 5 else None), refs[-4:]
    rows, taps, cols = k_hbm.shape
    sub, unroll = steps_of(rows)
    stream = Stream(k_hbm, ring, sem, sub * unroll)
    stream.start()
    time = u_ref.shape[1] // groups
    tap_start = pos_ref[1]
    sample = lax.broadcasted_iota(jnp.int32, (8, time), 0) + lax.broadcasted_iota(
        jnp.int32, (8, time), 1
    )
    acc_ref[...] = jnp.zeros_like(acc_ref) if before_ref is None else before_ref[...]

    def body(step, carry):
        slot = stream.next(step)
        for n in range(unroll):
            at = pl.multiple_of((step * unroll + n) * sub, sub)
            k = ring[slot, n * sub : (n + 1) * sub].reshape(sub * taps, cols)
            stacks = []
            for g in range(groups):
                u = u_ref[pl.ds(at, sub), g * time : (g + 1) * time].astype(f32)
                u = pltpu.roll(u, time - tap_start, 1)
                base = jnp.stack([pltpu.roll(u, time - i, 1) if i else u for i in range(8)], axis=1)
                terms = []
                for j in range(taps // 8):
                    moved = pltpu.roll(base, time - 8 * j, 2) if j else base
                    inside = (sample < time - tap_start - 8 * j)[None]
                    terms.append(jnp.where(inside, moved, 0.0))
                stacks.append(jnp.stack(terms, 1).astype(bf16).reshape(sub * taps, time))
            stacked = jnp.concatenate(stacks, axis=1)
            acc_ref[...] += lax.dot_general(
                stacked, k, (((0,), (0,)), ((), ())), preferred_element_type=f32
            )
        return carry

    lax.fori_loop(0, rows // (sub * unroll), body, 0)
    o_ref[...] = acc_ref[...].astype(o_ref.dtype)


def backward(pos, kept, up, before, groups, kind, after):
    _, taps, cols = kept.shape
    rows, width = up.shape
    more = [] if before is None else [before]
    return pl.pallas_call(
        functools.partial(backward_kernel, groups=groups, waits=len(after)),
        in_specs=[SM, ANY, VM] + [ANY] * len(after) + [VM] * len(more),
        out_specs=VM,
        out_shape=jax.ShapeDtypeStruct((width, cols), kind),
        scratch_shapes=[pltpu.VMEM((width, cols), f32)] + ring_of(rows, taps, cols),
        compiler_params=pltpu.CompilerParams(vmem_limit_bytes=40 * MIB),
        cost_estimate=pl.CostEstimate(
            flops=2 * rows * taps * cols * width, bytes_accessed=width * cols * 4, transcendentals=0
        ),
        name="backward",
    )(pos, pltpu.with_memory_space_constraint(kept, pltpu.HBM), up, *after, *more)


def shifted(x, axis, shift):
    n = lax.axis_size(axis)
    return lax.ppermute(x, axis, [(i, (i + shift) % n) for i in range(n)])


def gather(x, axis):
    n = lax.axis_size(axis)
    if n > 8:
        got = lax.all_gather(x, axis)
        return [got[i] for i in range(n)], [jnp.int32(i) for i in range(n)]
    me = lax.axis_index(axis)
    return [x] + [shifted(x, axis, k) for k in range(1, n)], [(me - k) % n for k in range(n)]


def ordered(parts):
    blocks, owners = parts
    if len(blocks) == 2:
        swap = owners[0] > 0
        return [jnp.where(swap, blocks[1], blocks[0]), jnp.where(swap, blocks[0], blocks[1])]
    stack, owners = jnp.stack(blocks), jnp.stack(owners)
    at = jnp.argsort(owners)
    return [lax.dynamic_index_in_dim(stack, at[i], 0, False) for i in range(len(blocks))]


def sum_over(x, axis):
    n = lax.axis_size(axis)
    if n & (n - 1):
        return lax.psum(x, axis)
    step = 1
    while step < n:
        x = x + lax.ppermute(x, axis, [(i, i ^ step) for i in range(n)])
        step *= 2
    return x


def scatter_parts(x, axis):
    n = lax.axis_size(axis)
    me = lax.axis_index(axis)
    if n == 1:
        return [x[0]]
    if n > 8:
        got = lax.all_to_all(x, axis, 0, 0, tiled=True)
        return [got[i] for i in range(n)]
    parts = [lax.dynamic_index_in_dim(x, me, 0, False)]
    for k in range(1, n):
        parts.append(shifted(lax.dynamic_index_in_dim(x, (me + k) % n, 0, False), axis, k))
    return parts


def total_of(parts):
    total = parts[0].astype(f32)
    for part in parts[1:]:
        total = total + part.astype(f32)
    return total


def on_device(response, onset, direct_wave, arrival):
    src_rows, tap_rows, rcv_rows = response.shape
    tile_time = direct_wave.shape[1]
    groups, src_n, tim_n = (lax.axis_size(a) for a in ("grp", "src", "tim"))
    g, s, r, c = (lax.axis_index(a) for a in ("grp", "src", "rcv", "tim"))
    time = src_n * tile_time
    width = groups * time
    rows = src_rows // groups
    part_time = tile_time // tim_n
    halves = 2 if rows % 32 == 0 and rows >= 64 else 1
    half = rows // halves
    share = half // tim_n

    def position(h):
        return jnp.stack([g * rows + h * half, c * tap_rows]).astype(jnp.int32)

    def whole_field(piece):
        if part_time % 16:
            field = piece
            for axis in ("grp", "src", "tim"):
                field = lax.all_gather(field, axis)
            field = field.transpose(2, 1, 0, 3, 4).reshape(1, width, rcv_rows)
            return [field], jnp.zeros((1,), jnp.int32)
        blocks, owners = gather(piece, "grp")
        pair = jnp.stack(blocks)
        where = jnp.stack([o * time for o in owners])
        blocks, owners = gather(pair, "src")
        line = jnp.concatenate(blocks)
        where = jnp.concatenate([where + o * tile_time for o in owners])
        blocks, owners = gather(line, "tim")
        where = jnp.concatenate([where + o * part_time for o in owners])
        return blocks, where.astype(jnp.int32)

    direct_piece = lax.dynamic_slice_in_dim(direct_wave, c * part_time, part_time, 1).T
    my_arrival = lax.dynamic_slice_in_dim(arrival, s * src_rows, src_rows).reshape(groups, rows)
    parts = scatter_parts(my_arrival, "grp")
    owners = [(g - k) % groups if groups <= 8 else jnp.int32(k) for k in range(groups)]
    src_arrival = jnp.stack(ordered((parts, owners)))
    rcv_arrival = lax.dynamic_slice_in_dim(arrival, r * rcv_rows, rcv_rows)

    blocks, where = whole_field(direct_piece)
    kept, energies, energy = [], [], None
    hops = ["tim", "rcv", "grp", "src"]

    def next_energy():
        nonlocal energy
        if not hops:
            return []
        energy = jnp.broadcast_to(sum(energies), (8, 128)) if energy is None else energy
        energy = sum_over(energy, hops.pop(0))
        return [energy]

    up_time = lax.broadcasted_iota(jnp.int32, (1, 1, time), 2)
    piece_time = s * tile_time + c * part_time
    piece_time = piece_time + lax.broadcasted_iota(jnp.int32, (part_time, 1), 0)

    for iteration in range(ITERS):
        final_pass = iteration + 1 == ITERS
        ups, totals, after = [], [], []
        for h in range(halves):
            if iteration == 0:
                partial, muted, squares = first_forward(
                    position(h), where, response, onset, blocks, half, width, after
                )
                kept.append(muted)
                energies.append(squares)
            else:
                partial = forward(position(h), where, kept[h], blocks, width, after)
            partial = partial.astype(bf16).reshape(tim_n, share, width)
            mine = total_of(scatter_parts(partial, "tim")).astype(bf16)
            after = [mine]
            got = gather(mine, "rcv")[0]
            got = got if len(got) == 2 else ordered(gather(mine, "rcv"))
            total = total_of(got).reshape(share, groups, time)
            limit = lax.dynamic_slice_in_dim(src_arrival, h * half + c * share, share, 1)
            total = jnp.where(up_time < limit.T[:, :, None], total, 0.0)
            totals.append(total)
            up = total.reshape(share, width).astype(bf16)
            ups.append(jnp.concatenate(ordered(gather(up, "tim"))))
        acc = None
        for h in range(halves):
            kind = bf16 if h + 1 == halves else f32
            after = (after if h == 0 else []) + next_energy()
            acc = backward(position(h), kept[h], ups[h], acc, groups, kind, after)
        if iteration == 0:
            while hops:
                next_energy()
            unit_gain = lax.rsqrt(energy[0, 0] / STATIONS + 1e-06)
        sums = acc.reshape(groups, src_n, tim_n, part_time, rcv_rows)
        sums = total_of(scatter_parts(sums.transpose(2, 0, 1, 3, 4), "tim")).astype(bf16)
        sums = total_of(scatter_parts(sums, "grp")).astype(bf16)
        sums = total_of(scatter_parts(sums, "src"))
        piece = (
            direct_piece.astype(f32)
            + jnp.where(piece_time < rcv_arrival[None, :], unit_gain * unit_gain * sums, 0.0)
        ).astype(bf16)
        if not final_pass:
            blocks, where = whole_field(piece)
    totals, _ = lax.optimization_barrier((totals, acc))
    out = jnp.stack([(unit_gain * t).astype(bf16) for t in totals])
    out = jnp.stack(ordered(gather(out, "tim")), 1).reshape(rows, groups, time).transpose(1, 0, 2)
    out = scatter_parts(out, "grp")
    focus_up = jnp.concatenate(ordered((out, owners)))
    focus_down = jnp.concatenate(ordered(gather(piece, "tim"))).T
    return (focus_down, focus_up)


def solution(mesh):
    in_specs = (P("src", "tim", "rcv"), P("src", "rcv"), P(("grp", "rcv"), "src"), P("grp"))
    out_specs = (P(("grp", "rcv"), "src"), P(("grp", "src"), None))
    return jax.shard_map(
        on_device, mesh=mesh, in_specs=in_specs, out_specs=out_specs, check_vma=False
    )
```

time: 308 us -> 244 us (0.79); the launches traced: 304 us -> 244 us
  local copies, waits for them, and re-layouts: 53.4 us -> 5.44 us
  other arithmetic: 11 us -> 3.26 us
  Pallas kernels: 139 us -> 135 us
    unnamed x40 -> x21, local copies, waits for them, and re-layouts: 44.4 us -> 2.74 us
    ppermute x43 -> x36, waiting for transfers between devices: 58.7 us -> 49.5 us  [shifted(): return lax.ppermute(x, axis, [(i, (i + shift) % n) for i in range(n)])]
    ppermute x0 -> x5, waiting for transfers between devices: none -> 8.67 us  [sum_over(): x = x + lax.ppermute(x, axis, [(i, i ^ step) for i in range(n)])]
    ppermute x43 -> x36, starting transfers between devices: 39.2 us -> 31.7 us  [shifted(): return lax.ppermute(x, axis, [(i, (i + shift) % n) for i in range(n)])]
    ppermute x0 -> x5, starting transfers between devices: none -> 6.45 us  [sum_over(): x = x + lax.ppermute(x, axis, [(i, i ^ step) for i in range(n)])]
    another operation x7 -> x9, other arithmetic: 3.96 us -> 0.27 us  [the longest x2 0.15 us: position(): return jnp.stack([g * rows + h * half, c * tap_rows]).astype(jnp.int32)]
    pallas_call x9 -> x8, Pallas kernels: 139 us -> 135 us  [the longest x4 70.6 us: backward(): pl.pallas_call(functools.partial(backward_kernel, groups=groups, waits=le...]
  transfers between devices with their start and end apart: 43 -> 41, of which waited for: 21 -> 31; matrix products, arithmetic and copies ran while one was open for 4% -> 2% of each run, Pallas kernels for 16% -> 14%
where the time goes in v2:
time: 244 us
  Pallas kernels  135 us (55%)
  waiting for transfers between devices  58.1 us (24%)
  starting transfers between devices  38.1 us (16%)
  local copies, waits for them, and re-layouts  5.44 us (2%)
  between operations  3.45 us (1%)
  other arithmetic  3.26 us (1%)
    pallas_call x4, Pallas kernels, backward(): pl.pallas_call(functools.partial(backward_kernel, groups=groups, waits=le...  70.6 us
    ppermute x36, waiting for transfers between devices, shifted(): return lax.ppermute(x, axis, [(i, (i + shift) % n) for i in range(n)])  49.5 us
    pallas_call x2, Pallas kernels, first_forward(): pl.pallas_call(functools.partial(first_kernel, groups=groups, waits=len(a...  34.9 us
    ppermute x36, starting transfers between devices, shifted(): return lax.ppermute(x, axis, [(i, (i + shift) % n) for i in range(n)])  31.7 us
    pallas_call x2, Pallas kernels, forward(): pl.pallas_call(functools.partial(forward_kernel, groups=groups, waits=len...  29.8 us
    ppermute x5, waiting for transfers between devices, sum_over(): x = x + lax.ppermute(x, axis, [(i, i ^ step) for i in range(n)])  8.67 us
    ppermute x5, starting transfers between devices, sum_over(): x = x + lax.ppermute(x, axis, [(i, i ^ step) for i in range(n)])  6.45 us
  transfers between devices with their start and end apart: 41, of which 31 were waited for; matrix products, arithmetic and copies ran while one was open for 2% of the time, Pallas kernels for 14%

profile of v2, /device:TPU:0, one launch (start us, length us, event | category | flops | bytes accessed | tf_op | source)
XLA Modules:
  0.0 243.7 jit_solution(609313921920199215)
XLA Ops:
  1.5 3.0 %collective-permute-start = (bf16[32,1024]{1,0:T(8,128)(2,1)S(1)}, bf16[32,1024]{1,0:T(8,128)(2,1)S(1)}, u32[]{:S(2)}, u32[]{:S(2)}) collective-permute-start(bf16[32,1024]{1,0:T(8,128)(2,1)S(1)} %dynamic-slice_bitcast_fusion.16), channel_id=1, source_target_pairs={{0,16},{16,0},{1,17},{17,1},{2,18},{18,2},{3,19},{19,3},{4,20},{20... | collective-permute-start | bytes 196616 | tf_op jit(solution)/shard_map/ppermute | solution.py:287
  8.8 2.6 %collective-permute-start.2 = (bf16[2,32,1024]{2,1,0:T(8,128)(2,1)S(1)}, bf16[2,32,1024]{2,1,0:T(8,128)(2,1)S(1)}, u32[]{:S(2)}, u32[]{:S(2)}) collective-permute-start(bf16[2,32,1024]{2,1,0:T(8,128)(2,1)S(1)} %pad_maximum_fusion.2), channel_id=1, source_target_pairs={{0,8},{4,12},{8,0},{12,4},{1,9},{5,13},{9,1},{13,5},{2,10},{6,14},... | collective-permute-start | bytes 393224 | tf_op jit(solution)/shard_map/ppermute | solution.py:287
  12.8 2.6 %collective-permute-done.1 = bf16[2,32,1024]{2,1,0:T(8,128)(2,1)S(1)} collective-permute-done((bf16[2,32,1024]{2,1,0:T(8,128)(2,1)S(1)}, bf16[2,32,1024]{2,1,0:T(8,128)(2,1)S(1)}, u32[]{:S(2)}, u32[]{:S(2)}) %collective-permute-start.1) | collective-permute-done | bytes 131104 | tf_op jit(solution)/shard_map/ppermute | solution.py:287
  15.4 3.8 %collective-permute-done.2 = bf16[2,32,1024]{2,1,0:T(8,128)(2,1)S(1)} collective-permute-done((bf16[2,32,1024]{2,1,0:T(8,128)(2,1)S(1)}, bf16[2,32,1024]{2,1,0:T(8,128)(2,1)S(1)}, u32[]{:S(2)}, u32[]{:S(2)}) %collective-permute-start.2) | collective-permute-done | bytes 131104 | tf_op jit(solution)/shard_map/ppermute | solution.py:287
  23.0 17.5 %first_forward.2 = (f32[128,512]{1,0:T(8,128)S(1)}, bf16[128,64,1024]{2,1,0:T(8,128)(2,1)}, f32[1]{0:T(128)}) custom-call(s32[2]{0:T(128)S(1)} %pad_add_fusion.pos_ref, s32[16]{0:T(128)S(1)} %pad_add_fusion.3.where_ref, bf16[512,64,1024]{2,1,0:T(8,128)(2,1)} %r_hbm.3, s32[512,1024]{1,0:T(8,128)S(1)} %copy-done, ...), custom_call_target="tpu_custom_call" | custom-call | flops 8589934592 | bytes 1048576 | tf_op jit(solution)/shard_map/first_forward/pallas_call | solution.py:184
  41.9 17.4 %first_forward.3 = (f32[128,512]{1,0:T(8,128)S(1)}, bf16[128,64,1024]{2,1,0:T(8,128)(2,1)}, f32[1]{0:T(128)}) custom-call(s32[2]{0:T(128)S(1)} %pad_add_fusion.4.pos_ref, s32[16]{0:T(128)S(1)} %pad_add_fusion.3.where_ref, bf16[512,64,1024]{2,1,0:T(8,128)(2,1)} %r_hbm.3, s32[512,1024]{1,0:T(8,128)S(1)} %copy-done.1, bf16[64,512]{1,0:T(8,128)(2,1)S(1)} %fusion.15.refs_0_, ...), custom_call_target="tpu_custom_call" | custom-call | flops 8589934592 | bytes 1048576 | tf_op jit(solution)/shard_map/first_forward/pallas_call | solution.py:184
  65.3 2.4 %collective-permute-done.13 = bf16[64,512]{1,0:T(8,128)(2,1)S(1)} collective-permute-done((bf16[64,512]{1,0:T(8,128)(2,1)S(1)}, bf16[64,512]{1,0:T(8,128)(2,1)S(1)}, u32[]{:S(2)}, u32[]{:S(2)}) %collective-permute-start.13) | collective-permute-done | bytes 65568 | tf_op jit(solution)/shard_map/ppermute | solution.py:287
  69.3 17.7 %backward.4.refs_1_ = f32[512,1024]{1,0:T(8,128)S(1)} custom-call(s32[2]{0:T(128)S(1)} %pad_add_fusion.pos_ref, bf16[128,64,1024]{2,1,0:T(8,128)(2,1)} %get-tuple-element.14.k_hbm, bf16[128,512]{1,0:T(8,128)(2,1)S(1)} %pad_maximum_fusion.4.u_ref, bf16[64,512]{1,0:T(8,128)(2,1)S(1)} %fusion.14.refs_0_, f32[8,128]{1,0:T(8,128)S(1)} %broadcast_add_fusion.refs_1_), custom_call_target="tpu_custom_call" | custom-call | flops 8589934592 | bytes 2097152 | tf_op jit(solution)/shard_map/backward/pallas_call | solution.py:271
  87.0 17.6 %backward.5 = bf16[512,1024]{1,0:T(8,128)(2,1)S(1)} custom-call(s32[2]{0:T(128)S(1)} %pad_add_fusion.4.pos_ref, bf16[128,64,1024]{2,1,0:T(8,128)(2,1)} %get-tuple-element.13.k_hbm, bf16[128,512]{1,0:T(8,128)(2,1)S(1)} %pad_maximum_fusion.3.u_ref, f32[8,128]{1,0:T(8,128)S(1)} %fusion.23.refs_0_, f32[512,1024]{1,0:T(8,128)S(1)} %backward.4.refs_1_), custom_call_target="tpu_custom_call" | custom-call | flops 8589934592 | bytes 2097152 | tf_op jit(solution)/shard_map/backward/pallas_call | solution.py:271
  109.1 6.6 %collective-permute-done.8 = f32[8,128]{1,0:T(8,128)S(1)} collective-permute-done((f32[8,128]{1,0:T(8,128)S(1)}, f32[8,128]{1,0:T(8,128)S(1)}, u32[]{:S(2)}, u32[]{:S(2)}) %collective-permute-start.8) | collective-permute-done | bytes 4128 | tf_op jit(solution)/shard_map/ppermute | solution.py:315
  115.7 3.2 %collective-permute-start.9 = (f32[8,128]{1,0:T(8,128)S(1)}, f32[8,128]{1,0:T(8,128)S(1)}, u32[]{:S(2)}, u32[]{:S(2)}) collective-permute-start(f32[8,128]{1,0:T(8,128)S(1)} %add.357), channel_id=1, source_target_pairs={{0,4},{4,0},{8,12},{12,8},{1,5},{5,1},{9,13},{13,9},{2,6},{6,2},{1... | collective-permute-start | bytes 12296 | tf_op jit(solution)/shard_map/ppermute | solution.py:315
  122.2 2.9 %collective-permute-start.21 = (bf16[32,1024]{1,0:T(8,128)(2,1)S(1)}, bf16[32,1024]{1,0:T(8,128)(2,1)S(1)}, u32[]{:S(2)}, u32[]{:S(2)}) collective-permute-start(bf16[32,1024]{1,0:T(8,128)(2,1)S(1)} %get-tuple-element.38), channel_id=1, source_target_pairs={{0,12},{4,0},{8,4},{12,8},{1,13},{5,1},{9,5},{13,9},{2,14},{6,2},{... | collective-permute-start | bytes 196616 | tf_op jit(solution)/shard_map/ppermute | solution.py:287
  127.2 3.0 %collective-permute-done.20 = bf16[32,1024]{1,0:T(8,128)(2,1)S(1)} collective-permute-done((bf16[32,1024]{1,0:T(8,128)(2,1)S(1)}, bf16[32,1024]{1,0:T(8,128)(2,1)S(1)}, u32[]{:S(2)}, u32[]{:S(2)}) %collective-permute-start.20) | collective-permute-done | bytes 65568 | tf_op jit(solution)/shard_map/ppermute | solution.py:287
  133.4 2.8 %collective-permute-done.22 = bf16[32,1024]{1,0:T(8,128)(2,1)S(1)} collective-permute-done((bf16[32,1024]{1,0:T(8,128)(2,1)S(1)}, bf16[32,1024]{1,0:T(8,128)(2,1)S(1)}, u32[]{:S(2)}, u32[]{:S(2)}) %collective-permute-start.22) | collective-permute-done | bytes 65568 | tf_op jit(solution)/shard_map/ppermute | solution.py:287
  136.9 3.2 %collective-permute-start.25 = (bf16[2,32,1024]{2,1,0:T(8,128)(2,1)S(1)}, bf16[2,32,1024]{2,1,0:T(8,128)(2,1)S(1)}, u32[]{:S(2)}, u32[]{:S(2)}) collective-permute-start(bf16[2,32,1024]{2,1,0:T(8,128)(2,1)S(1)} %pad_maximum_fusion.5), channel_id=1, source_target_pairs={{0,12},{4,0},{8,4},{12,8},{1,13},{5,1},{9,5},{13,9},{2,14},{6,2},{... | collective-permute-start | bytes 393224 | tf_op jit(solution)/shard_map/ppermute | solution.py:287
  140.1 3.1 %collective-permute-done.23 = bf16[2,32,1024]{2,1,0:T(8,128)(2,1)S(1)} collective-permute-done((bf16[2,32,1024]{2,1,0:T(8,128)(2,1)S(1)}, bf16[2,32,1024]{2,1,0:T(8,128)(2,1)S(1)}, u32[]{:S(2)}, u32[]{:S(2)}) %collective-permute-start.23) | collective-permute-done | bytes 131104 | tf_op jit(solution)/shard_map/ppermute | solution.py:287
  147.4 14.9 %forward.2 = f32[128,512]{1,0:T(8,128)S(1)} custom-call(s32[2]{0:T(128)S(1)} %pad_add_fusion.pos_ref, s32[16]{0:T(128)S(1)} %pad_add_fusion.3.where_ref, bf16[128,64,1024]{2,1,0:T(8,128)(2,1)} %get-tuple-element.14.k_hbm, bf16[8,32,1024]{2,1,0:T(8,128)(2,1)S(1)} %constant_dynamic-update-slice_fusion.5.refs_0_.refs_1_, ...), custom_call_target="tpu_custom_call" | custom-call | flops 8589934592 | bytes 1048576 | tf_op jit(solution)/shard_map/forward/pallas_call | solution.py:213
  163.7 14.9 %forward.3 = f32[128,512]{1,0:T(8,128)S(1)} custom-call(s32[2]{0:T(128)S(1)} %pad_add_fusion.4.pos_ref, s32[16]{0:T(128)S(1)} %pad_add_fusion.3.where_ref, bf16[128,64,1024]{2,1,0:T(8,128)(2,1)} %get-tuple-element.13.k_hbm, bf16[64,512]{1,0:T(8,128)(2,1)S(1)} %fusion.10.refs_0_, bf16[8,32,1024]{2,1,0:T(8,128)(2,1)S(1)} %constant_dynamic-update-slice_fusion.5.refs_0_.refs_1_, ...), custom_call_target="tpu_custom_call" | custom-call | flops 8589934592 | bytes 1048576 | tf_op jit(solution)/shard_map/forward/pallas_call | solution.py:213
  181.0 2.6 %collective-permute-done.31 = bf16[64,512]{1,0:T(8,128)(2,1)S(1)} collective-permute-done((bf16[64,512]{1,0:T(8,128)(2,1)S(1)}, bf16[64,512]{1,0:T(8,128)(2,1)S(1)}, u32[]{:S(2)}, u32[]{:S(2)}) %collective-permute-start.31) | collective-permute-done | bytes 65568 | tf_op jit(solution)/shard_map/ppermute | solution.py:287
  185.0 17.7 %backward.6.refs_0_ = f32[512,1024]{1,0:T(8,128)S(1)} custom-call(s32[2]{0:T(128)S(1)} %pad_add_fusion.pos_ref, bf16[128,64,1024]{2,1,0:T(8,128)(2,1)} %get-tuple-element.14.k_hbm, bf16[128,512]{1,0:T(8,128)(2,1)S(1)} %pad_maximum_fusion.7.u_ref, bf16[64,512]{1,0:T(8,128)(2,1)S(1)} %fusion.9.refs_0_), custom_call_target="tpu_custom_call" | custom-call | flops 8589934592 | bytes 2097152 | tf_op jit(solution)/shard_map/backward/pallas_call | solution.py:271
  202.8 17.6 %backward.7 = bf16[512,1024]{1,0:T(8,128)(2,1)S(1)} custom-call(s32[2]{0:T(128)S(1)} %pad_add_fusion.4.pos_ref, bf16[128,64,1024]{2,1,0:T(8,128)(2,1)} %get-tuple-element.13.k_hbm, bf16[128,512]{1,0:T(8,128)(2,1)S(1)} %pad_maximum_fusion.6.u_ref, f32[512,1024]{1,0:T(8,128)S(1)} %backward.6.refs_0_), custom_call_target="tpu_custom_call" | custom-call | flops 8589934592 | bytes 2097152 | tf_op jit(solution)/shard_map/backward/pallas_call | solution.py:271
  225.0 7.0 %collective-permute-done.34 = bf16[4,32,1024]{2,1,0:T(8,128)(2,1)S(1)} collective-permute-done((bf16[4,32,1024]{2,1,0:T(8,128)(2,1)S(1)}, bf16[4,32,1024]{2,1,0:T(8,128)(2,1)S(1)}, u32[]{:S(2)}, u32[]{:S(2)}) %collective-permute-start.34) | collective-permute-done | bytes 262176 | tf_op jit(solution)/shard_map/ppermute | solution.py:287
  232.1 2.6 %collective-permute-start.37 = (bf16[32,1024]{1,0:T(8,128)(2,1)S(1)}, bf16[32,1024]{1,0:T(8,128)(2,1)S(1)}, u32[]{:S(2)}, u32[]{:S(2)}) collective-permute-start(bf16[32,1024]{1,0:T(8,128)(2,1)S(1)} %get-tuple-element.35), channel_id=1, source_target_pairs={{0,12},{4,0},{8,4},{12,8},{1,13},{5,1},{9,5},{13,9},{2,14},{6,2},{... | collective-permute-start | bytes 196616 | tf_op jit(solution)/shard_map/ppermute | solution.py:287
  236.5 3.7 %collective-permute-done.36 = bf16[32,1024]{1,0:T(8,128)(2,1)S(1)} collective-permute-done((bf16[32,1024]{1,0:T(8,128)(2,1)S(1)}, bf16[32,1024]{1,0:T(8,128)(2,1)S(1)}, u32[]{:S(2)}, u32[]{:S(2)}) %collective-permute-start.36) | collective-permute-done | bytes 65568 | tf_op jit(solution)/shard_map/ppermute | solution.py:287
  (161 shorter events, 49.8 us)
Async XLA Ops:
  1.5 5.2 %collective-permute-start = (bf16[32,1024]{1,0:T(8,128)(2,1)S(1)}, bf16[32,1024]{1,0:T(8,128)(2,1)S(1)}, u32[]{:S(2)}, u32[]{:S(2)}) collective-permute-start(bf16[32,1024]{1,0:T(8,128)(2,1)S(1)} %dynamic-slice_bitcast_fusion.16), channel_id=1, source_target_pairs={{0,16},{16,0},{1,17},{17,1},{2,18},{18,2},{3,19},{19,3},{4,20},{20... | collective-permute-start | bytes 196616 | tf_op jit(solution)/shard_map/ppermute | solution.py:287
  5.2 35.5 %collective-permute-start.11 = (s32[256]{0:T(256)S(1)}, s32[256]{0:T(256)S(1)}, u32[]{:S(2)}, u32[]{:S(2)}) collective-permute-start(s32[256]{0:T(256)S(1)} %bitcast.160), channel_id=1, source_target_pairs={{0,16},{16,0},{1,17},{17,1},{2,18},{18,2},{3,19},{19,3},{4,20},{20... | collective-permute-start | bytes 3080 | tf_op jit(solution)/shard_map/ppermute | solution.py:287
  6.7 8.7 %collective-permute-start.1 = (bf16[2,32,1024]{2,1,0:T(8,128)(2,1)S(1)}, bf16[2,32,1024]{2,1,0:T(8,128)(2,1)S(1)}, u32[]{:S(2)}, u32[]{:S(2)}) collective-permute-start(bf16[2,32,1024]{2,1,0:T(8,128)(2,1)S(1)} %pad_maximum_fusion.2), channel_id=1, source_target_pairs={{0,4},{4,8},{8,12},{12,0},{1,5},{5,9},{9,13},{13,1},{2,6},{6,10},{... | collective-permute-start | bytes 393224 | tf_op jit(solution)/shard_map/ppermute | solution.py:287
  8.8 10.4 %collective-permute-start.2 = (bf16[2,32,1024]{2,1,0:T(8,128)(2,1)S(1)}, bf16[2,32,1024]{2,1,0:T(8,128)(2,1)S(1)}, u32[]{:S(2)}, u32[]{:S(2)}) collective-permute-start(bf16[2,32,1024]{2,1,0:T(8,128)(2,1)S(1)} %pad_maximum_fusion.2), channel_id=1, source_target_pairs={{0,8},{4,12},{8,0},{12,4},{1,9},{5,13},{9,1},{13,5},{2,10},{6,14},... | collective-permute-start | bytes 393224 | tf_op jit(solution)/shard_map/ppermute | solution.py:287
  11.4 8.0 %collective-permute-start.3 = (bf16[2,32,1024]{2,1,0:T(8,128)(2,1)S(1)}, bf16[2,32,1024]{2,1,0:T(8,128)(2,1)S(1)}, u32[]{:S(2)}, u32[]{:S(2)}) collective-permute-start(bf16[2,32,1024]{2,1,0:T(8,128)(2,1)S(1)} %pad_maximum_fusion.2), channel_id=1, source_target_pairs={{0,12},{4,0},{8,4},{12,8},{1,13},{5,1},{9,5},{13,9},{2,14},{6,2},{... | collective-permute-start | bytes 393224 | tf_op jit(solution)/shard_map/ppermute | solution.py:287
  60.1 5.1 %collective-permute-start.15 = (bf16[64,512]{1,0:T(8,128)(2,1)S(1)}, bf16[64,512]{1,0:T(8,128)(2,1)S(1)}, u32[]{:S(2)}, u32[]{:S(2)}) collective-permute-start(bf16[64,512]{1,0:T(8,128)(2,1)S(1)} %fusion.15.refs_0_), channel_id=1, source_target_pairs={{0,2},{2,0},{1,3},{3,1},{4,6},{6,4},{5,7},{7,5},{8,10},{10,8},{9,1... | collective-permute-start | bytes 196616 | tf_op jit(solution)/shard_map/ppermute | solution.py:287
  63.2 4.5 %collective-permute-start.13 = (bf16[64,512]{1,0:T(8,128)(2,1)S(1)}, bf16[64,512]{1,0:T(8,128)(2,1)S(1)}, u32[]{:S(2)}, u32[]{:S(2)}) collective-permute-start(bf16[64,512]{1,0:T(8,128)(2,1)S(1)} %fusion.14.refs_0_), channel_id=1, source_target_pairs={{0,2},{2,0},{1,3},{3,1},{4,6},{6,4},{5,7},{7,5},{8,10},{10,8},{9,1... | collective-permute-start | bytes 196616 | tf_op jit(solution)/shard_map/ppermute | solution.py:287
  107.0 15.1 %collective-permute-start.18 = (bf16[4,32,1024]{2,1,0:T(8,128)(2,1)S(1)}, bf16[4,32,1024]{2,1,0:T(8,128)(2,1)S(1)}, u32[]{:S(2)}, u32[]{:S(2)}) collective-permute-start(bf16[4,32,1024]{2,1,0:T(8,128)(2,1)S(1)} %dynamic-slice_bitcast_fusion.3), channel_id=1, source_target_pairs={{0,16},{16,0},{1,17},{17,1},{2,18},{18,2},{3,19},{19,3},{4,20},{20... | collective-permute-start | bytes 786440 | tf_op jit(solution)/shard_map/ppermute | solution.py:287
  108.6 7.1 %collective-permute-start.8 = (f32[8,128]{1,0:T(8,128)S(1)}, f32[8,128]{1,0:T(8,128)S(1)}, u32[]{:S(2)}, u32[]{:S(2)}) collective-permute-start(f32[8,128]{1,0:T(8,128)S(1)} %fusion.23.refs_0_), channel_id=1, source_target_pairs={{0,16},{16,0},{1,17},{17,1},{2,18},{18,2},{3,19},{19,3},{4,20},{20... | collective-permute-start | bytes 12296 | tf_op jit(solution)/shard_map/ppermute | solution.py:315
  115.7 4.8 %collective-permute-start.9 = (f32[8,128]{1,0:T(8,128)S(1)}, f32[8,128]{1,0:T(8,128)S(1)}, u32[]{:S(2)}, u32[]{:S(2)}) collective-permute-start(f32[8,128]{1,0:T(8,128)S(1)} %add.357), channel_id=1, source_target_pairs={{0,4},{4,0},{8,12},{12,8},{1,5},{5,1},{9,13},{13,9},{2,6},{6,2},{1... | collective-permute-start | bytes 12296 | tf_op jit(solution)/shard_map/ppermute | solution.py:315
  120.5 5.3 %collective-permute-start.10 = (f32[8,128]{1,0:T(8,128)S(1)}, f32[8,128]{1,0:T(8,128)S(1)}, u32[]{:S(2)}, u32[]{:S(2)}) collective-permute-start(f32[8,128]{1,0:T(8,128)S(1)} %add.358), channel_id=1, source_target_pairs={{0,8},{4,12},{8,0},{12,4},{1,9},{5,13},{9,1},{13,5},{2,10},{6,14},... | collective-permute-start | bytes 12296 | tf_op jit(solution)/shard_map/ppermute | solution.py:315
  122.2 5.0 %collective-permute-start.21 = (bf16[32,1024]{1,0:T(8,128)(2,1)S(1)}, bf16[32,1024]{1,0:T(8,128)(2,1)S(1)}, u32[]{:S(2)}, u32[]{:S(2)}) collective-permute-start(bf16[32,1024]{1,0:T(8,128)(2,1)S(1)} %get-tuple-element.38), channel_id=1, source_target_pairs={{0,12},{4,0},{8,4},{12,8},{1,13},{5,1},{9,5},{13,9},{2,14},{6,2},{... | collective-permute-start | bytes 196616 | tf_op jit(solution)/shard_map/ppermute | solution.py:287
  125.0 5.2 %collective-permute-start.20 = (bf16[32,1024]{1,0:T(8,128)(2,1)S(1)}, bf16[32,1024]{1,0:T(8,128)(2,1)S(1)}, u32[]{:S(2)}, u32[]{:S(2)}) collective-permute-start(bf16[32,1024]{1,0:T(8,128)(2,1)S(1)} %get-tuple-element.39), channel_id=1, source_target_pairs={{0,8},{4,12},{8,0},{12,4},{1,9},{5,13},{9,1},{13,5},{2,10},{6,14},... | collective-permute-start | bytes 196616 | tf_op jit(solution)/shard_map/ppermute | solution.py:287
  125.7 6.1 %collective-permute-start.19 = (bf16[32,1024]{1,0:T(8,128)(2,1)S(1)}, bf16[32,1024]{1,0:T(8,128)(2,1)S(1)}, u32[]{:S(2)}, u32[]{:S(2)}) collective-permute-start(bf16[32,1024]{1,0:T(8,128)(2,1)S(1)} %get-tuple-element.37), channel_id=1, source_target_pairs={{0,4},{4,8},{8,12},{12,0},{1,5},{5,9},{9,13},{13,1},{2,6},{6,10},{... | collective-permute-start | bytes 196616 | tf_op jit(solution)/shard_map/ppermute | solution.py:287
  136.2 7.0 %collective-permute-start.23 = (bf16[2,32,1024]{2,1,0:T(8,128)(2,1)S(1)}, bf16[2,32,1024]{2,1,0:T(8,128)(2,1)S(1)}, u32[]{:S(2)}, u32[]{:S(2)}) collective-permute-start(bf16[2,32,1024]{2,1,0:T(8,128)(2,1)S(1)} %pad_maximum_fusion.5), channel_id=1, source_target_pairs={{0,4},{4,8},{8,12},{12,0},{1,5},{5,9},{9,13},{13,1},{2,6},{6,10},{... | collective-permute-start | bytes 393224 | tf_op jit(solution)/shard_map/ppermute | solution.py:287
  136.3 9.1 %collective-permute-start.24 = (bf16[2,32,1024]{2,1,0:T(8,128)(2,1)S(1)}, bf16[2,32,1024]{2,1,0:T(8,128)(2,1)S(1)}, u32[]{:S(2)}, u32[]{:S(2)}) collective-permute-start(bf16[2,32,1024]{2,1,0:T(8,128)(2,1)S(1)} %pad_maximum_fusion.5), channel_id=1, source_target_pairs={{0,8},{4,12},{8,0},{12,4},{1,9},{5,13},{9,1},{13,5},{2,10},{6,14},... | collective-permute-start | bytes 393224 | tf_op jit(solution)/shard_map/ppermute | solution.py:287
  136.9 8.5 %collective-permute-start.25 = (bf16[2,32,1024]{2,1,0:T(8,128)(2,1)S(1)}, bf16[2,32,1024]{2,1,0:T(8,128)(2,1)S(1)}, u32[]{:S(2)}, u32[]{:S(2)}) collective-permute-start(bf16[2,32,1024]{2,1,0:T(8,128)(2,1)S(1)} %pad_maximum_fusion.5), channel_id=1, source_target_pairs={{0,12},{4,0},{8,4},{12,8},{1,13},{5,1},{9,5},{13,9},{2,14},{6,2},{... | collective-permute-start | bytes 393224 | tf_op jit(solution)/shard_map/ppermute | solution.py:287
  178.9 4.8 %collective-permute-start.31 = (bf16[64,512]{1,0:T(8,128)(2,1)S(1)}, bf16[64,512]{1,0:T(8,128)(2,1)S(1)}, u32[]{:S(2)}, u32[]{:S(2)}) collective-permute-start(bf16[64,512]{1,0:T(8,128)(2,1)S(1)} %fusion.10.refs_0_), channel_id=1, source_target_pairs={{0,2},{2,0},{1,3},{3,1},{4,6},{6,4},{5,7},{7,5},{8,10},{10,8},{9,1... | collective-permute-start | bytes 196616 | tf_op jit(solution)/shard_map/ppermute | solution.py:287
  180.0 4.6 %collective-permute-start.29 = (bf16[64,512]{1,0:T(8,128)(2,1)S(1)}, bf16[64,512]{1,0:T(8,128)(2,1)S(1)}, u32[]{:S(2)}, u32[]{:S(2)}) collective-permute-start(bf16[64,512]{1,0:T(8,128)(2,1)S(1)} %fusion.9.refs_0_), channel_id=1, source_target_pairs={{0,2},{2,0},{1,3},{3,1},{4,6},{6,4},{5,7},{7,5},{8,10},{10,8},{9,1... | collective-permute-start | bytes 196616 | tf_op jit(solution)/shard_map/ppermute | solution.py:287
  184.7 18.1 %collective-permute-start.30 = (bf16[64,512]{1,0:T(8,128)(2,1)S(1)}, bf16[64,512]{1,0:T(8,128)(2,1)S(1)}, u32[]{:S(2)}, u32[]{:S(2)}) collective-permute-start(bf16[64,512]{1,0:T(8,128)(2,1)S(1)} %get-tuple-element.41), channel_id=1, source_target_pairs={{0,1},{1,0},{2,3},{3,2},{4,5},{5,4},{6,7},{7,6},{8,9},{9,8},{10,11... | collective-permute-start | bytes 196616 | tf_op jit(solution)/shard_map/ppermute | solution.py:287
  222.8 9.2 %collective-permute-start.34 = (bf16[4,32,1024]{2,1,0:T(8,128)(2,1)S(1)}, bf16[4,32,1024]{2,1,0:T(8,128)(2,1)S(1)}, u32[]{:S(2)}, u32[]{:S(2)}) collective-permute-start(bf16[4,32,1024]{2,1,0:T(8,128)(2,1)S(1)} %dynamic-slice_bitcast_fusion.2), channel_id=1, source_target_pairs={{0,16},{16,0},{1,17},{17,1},{2,18},{18,2},{3,19},{19,3},{4,20},{20... | collective-permute-start | bytes 786440 | tf_op jit(solution)/shard_map/ppermute | solution.py:287
  224.4 11.1 %collective-permute-start.40 = (bf16[256,256]{1,0:T(8,128)(2,1)S(1)}, bf16[256,256]{1,0:T(8,128)(2,1)S(1)}, u32[]{:S(2)}, u32[]{:S(2)}) collective-permute-start(bf16[256,256]{1,0:T(8,128)(2,1)S(1)} %dynamic-slice_bitcast_fusion.4), channel_id=1, source_target_pairs={{0,16},{16,0},{1,17},{17,1},{2,18},{18,2},{3,19},{19,3},{4,20},{20... | collective-permute-start | bytes 393224 | tf_op jit(solution)/shard_map/ppermute | solution.py:287
  234.6 5.7 %collective-permute-start.36 = (bf16[32,1024]{1,0:T(8,128)(2,1)S(1)}, bf16[32,1024]{1,0:T(8,128)(2,1)S(1)}, u32[]{:S(2)}, u32[]{:S(2)}) collective-permute-start(bf16[32,1024]{1,0:T(8,128)(2,1)S(1)} %get-tuple-element.36), channel_id=1, source_target_pairs={{0,8},{4,12},{8,0},{12,4},{1,9},{5,13},{9,1},{13,5},{2,10},{6,14},... | collective-permute-start | bytes 196616 | tf_op jit(solution)/shard_map/ppermute | solution.py:287
  235.5 6.1 %collective-permute-start.35 = (bf16[32,1024]{1,0:T(8,128)(2,1)S(1)}, bf16[32,1024]{1,0:T(8,128)(2,1)S(1)}, u32[]{:S(2)}, u32[]{:S(2)}) collective-permute-start(bf16[32,1024]{1,0:T(8,128)(2,1)S(1)} %get-tuple-element.34), channel_id=1, source_target_pairs={{0,4},{4,8},{8,12},{12,0},{1,5},{5,9},{9,13},{13,1},{2,6},{6,10},{... | collective-permute-start | bytes 196616 | tf_op jit(solution)/shard_map/ppermute | solution.py:287
  (21 other events, 142.0 us)
